TPU v7x, 512 devices: a whole 4x8x8 slice. The times are simulated.
512 devices in a mesh: dom: 64 (over y, x, z_lo), rel: 8 (over z_hi, core).
Axes of the slice: x: 4, y: 8, z: 8 (z_hi: 4, z_lo: 2; z = z_hi * 2 + z_lo), core: 2. Of those that a mesh axis runs over, the one named last changes fastest.
Arguments:
- embeddings: bfloat16 [65536, 256], P(('dom', 'rel')), may hold values from -4 to 4
- relations: float32 [8192, 256], P('rel'), may hold values from -6 to 6
- lhs_ids: int32 [64, 8, 512], P('dom', 'rel'), may hold values from 0 to 1023
- rhs_ids: int32 [64, 8, 512], P('dom', 'rel'), may hold values from 0 to 1023
- rel_ids: int32 [64, 8, 512], P('dom', 'rel'), may hold values from 0 to 1023
- neg_ids: int32 [64, 8, 1, 2048], P('dom', 'rel'), may hold values from 0 to 1023
- live: int32 [512], P(('dom', 'rel')), may hold values from 1 to 512, 131072 in all
Outputs:
- entity_grad: float32 [65536, 256], P(('dom', 'rel'))
- relation_grad: float32 [8192, 256], P('rel')
Inputs may be any that keep to these rules, and one draw needn't show every extreme that they name: Slots of a device below its live count hold its live edges; the others add nothing.
All inputs are finite; a program needn't handle non-finite values.
Results may differ from a plain program's by a relative error of at most 0.009.
Values may be sent and summed in bfloat16 or wider, within the bound.
No kernel may reach another device: no remote copies, remote signals or barrier semaphores. Data moves between devices by JAX's collectives and lax.ppermute only.
A program may use at most 64 MiB of HBM per device.

v0:
```python
import jax
import jax.numpy as jnp
from jax import lax
from jax.sharding import PartitionSpec as P


def from_behind(block, axis, distance):
    devices = range(lax.axis_size(axis))
    route = [((i - distance) % len(devices), i) for i in devices]
    return lax.ppermute(block, axis, route)


def complex_split(values):
    width = values.shape[-1] // 2
    return (values[..., :width], values[..., width:])


def edge_terms(
    own_block, partner_block, rel_table, lhs_index, rhs_index, rel_index, neg_index, live_count
):
    edge_count = lhs_index.shape[0]
    blocks, negatives = neg_index.shape
    weight = negatives ** (-0.5)
    alive_mask = (jnp.arange(edge_count) < live_count).astype(jnp.float32)
    head_rows = own_block[lhs_index].astype(jnp.float32)
    tail_rows = partner_block[rhs_index].astype(jnp.float32)
    rel_rows = rel_table[rel_index]
    head_real, head_imag = complex_split(head_rows)
    rel_real, rel_imag = complex_split(rel_rows)
    query_vec = jnp.concatenate(
        [head_real * rel_real - head_imag * rel_imag, head_real * rel_imag + head_imag * rel_real],
        axis=-1,
    ).astype(jnp.bfloat16)
    query_wide = query_vec.astype(jnp.float32)
    pos_score = jnp.sum(query_wide * tail_rows, axis=-1)
    pos_grad = -jax.nn.sigmoid(-pos_score) * alive_mask
    partner_grad = (
        jnp.zeros(partner_block.shape, jnp.float32)
        .at[rhs_index]
        .add(pos_grad[:, None] * query_wide)
    )
    neg_rows = partner_block[neg_index[0]]
    scores = lax.dot_general(
        query_vec, neg_rows, (((1,), (1,)), ((), ())), preferred_element_type=jnp.float32
    )
    neg_grad = (jax.nn.sigmoid(scores) * (weight * alive_mask)[:, None]).astype(jnp.bfloat16)
    neg_parts = jnp.dot(neg_grad, neg_rows, preferred_element_type=jnp.float32)
    row_grad = lax.dot_general(
        neg_grad, query_vec, (((0,), (0,)), ((), ())), preferred_element_type=jnp.float32
    )
    partner_grad = partner_grad.at[neg_index[0]].add(row_grad)
    query_grad = pos_grad[:, None] * tail_rows + neg_parts
    grad_real, grad_imag = complex_split(query_grad)
    head_grad = jnp.concatenate(
        [grad_real * rel_real + grad_imag * rel_imag, grad_imag * rel_real - grad_real * rel_imag],
        axis=-1,
    )
    rel_term = jnp.concatenate(
        [
            grad_real * head_real + grad_imag * head_imag,
            grad_imag * head_real - grad_real * head_imag,
        ],
        axis=-1,
    )
    own_grad = jnp.zeros(own_block.shape, jnp.float32).at[lhs_index].add(head_grad)
    rel_partial = jnp.zeros(rel_table.shape, jnp.float32).at[rel_index].add(rel_term)
    return (own_grad, partner_grad, rel_partial)


def local(embeddings, relations, lhs_ids, rhs_ids, rel_ids, neg_ids, live):
    half_way = lax.axis_size("dom") // 2
    own_block = lax.all_gather(embeddings, "rel", axis=0, tiled=True)
    partner_block = from_behind(own_block, "dom", half_way)
    own_grad, partner_grad, rel_partial = edge_terms(
        own_block,
        partner_block,
        relations,
        lhs_ids[0, 0],
        rhs_ids[0, 0],
        rel_ids[0, 0],
        neg_ids[0, 0],
        live[0],
    )
    rel_total = lax.psum(rel_partial, "dom")
    own_round = own_grad.astype(jnp.bfloat16)
    partner_round = partner_grad.astype(jnp.bfloat16)
    returned = from_behind(partner_round, "dom", -half_way)
    own_sum, back_sum = (
        lax.psum_scatter(own_round, "rel", scatter_dimension=0, tiled=True).astype(jnp.float32),
        lax.psum_scatter(returned, "rel", scatter_dimension=0, tiled=True).astype(jnp.float32),
    )
    return (own_sum + back_sum, rel_total)


def solution(mesh):
    placed = (
        P(("dom", "rel"), None),
        P("rel", None),
        P("dom", "rel", None),
        P("dom", "rel", None),
        P("dom", "rel", None),
        P("dom", "rel", None, None),
        P(("dom", "rel")),
    )
    return jax.shard_map(
        local,
        mesh=mesh,
        in_specs=placed,
        out_specs=(P(("dom", "rel"), None), P("rel", None)),
        check_vma=False,
    )
```

profile of v0, /device:TPU:2, one launch (start us, length us, event | category | flops | bytes accessed | tf_op | source)
XLA Modules:
  0.0 758.9 jit_solution(10587431559341063056)
XLA Ops:
  8.1 21.1 %all_gather.3 = bf16[1024,256]{1,0:T(8,128)(2,1)S(1)} all-gather(bf16[128,256]{1,0:T(8,128)(2,1)} %param.7), channel_id=1, replica_groups=mesh['dom'=64,'rel'=8] {'rel'}, dimensions={0}, use_global_device_ids=true | all-gather | bytes 589824 | tf_op jit(solution)/shard_map/all_gather | solution.py:72
  29.2 7.7 %collective-permute-start = (bf16[1024,256]{1,0:T(8,128)(2,1)S(1)}, bf16[1024,256]{1,0:T(8,128)(2,1)S(1)}, u32[]{:S(2)}, u32[]{:S(2)}) collective-permute-start(bf16[1024,256]{1,0:T(8,128)(2,1)S(1)} %all_gather.3), channel_id=1, source_target_pairs={{256,0},{264,8},{272,16},{280,24},{288,32},{296,40},{304,48},{312,... | collective-permute-start | bytes 1572872 | tf_op jit(solution)/shard_map/ppermute | solution.py:10
  38.3 1.6 gather_fusion.1
  41.3 2.0 gather_fusion
  43.7 1.1 copy.21
  44.9 15.0 %collective-permute-done = bf16[1024,256]{1,0:T(8,128)(2,1)S(1)} collective-permute-done((bf16[1024,256]{1,0:T(8,128)(2,1)S(1)}, bf16[1024,256]{1,0:T(8,128)(2,1)S(1)}, u32[]{:S(2)}, u32[]{:S(2)}) %collective-permute-start) | collective-permute-done | bytes 524320 | tf_op jit(solution)/shard_map/ppermute | solution.py:10
  59.8 1.9 gather_fusion.2
  62.0 9.0 %gather_fusion.3 = bf16[2048,256]{1,0:T(8,128)(2,1)} fusion(bf16[1024,256]{1,0:T(8,128)(2,1)S(1)} %collective-permute-done, s32[2048]{0:T(1024)S(1)} %broadcast_clamp_fusion), kind=kCustom, calls=%fused_computation.3 | custom fusion | bytes 2105344 | tf_op jit(solution)/shard_map/gather | solution.py:42
  71.1 2.9 multiply_convert_fusion
  74.1 1.5 fusion.1
  75.9 1.0 copy.17
  76.9 4.0 scatter_custom_fusion
  80.9 0.8 convert_element_type.30
  82.2 3.6 scatter_custom_fusion.1
  85.8 3.6 fusion.9
  89.5 12.4 %scatter_fusion = f32[1024,256]{1,0:T(8,128)S(1)} fusion(f32[1024,256]{1,0:T(8,128)S(1)} %scatter_custom_fusion.1, s32[2048]{0:T(1024)S(1)} %bitcast.20, f32[2048,256]{1,0:T(8,128)} %fusion.9), kind=kCustom, calls=%fused_computation.6 | custom fusion | flops 524288 | bytes 6299648 | tf_op jit(solution)/shard_map/scatter-add | solution.py:51
  101.9 8.3 %collective-permute-start.1 = (bf16[1024,256]{1,0:T(8,128)(2,1)S(1)}, bf16[1024,256]{1,0:T(8,128)(2,1)S(1)}, u32[]{:S(2)}, u32[]{:S(2)}) collective-permute-start(bf16[1024,256]{1,0:T(8,128)(2,1)S(1)} %convert_element_type.32), channel_id=1, source_target_pairs={{256,0},{264,8},{272,16},{280,24},{288,32},{296,40},{304,48},{312,... | collective-permute-start | bytes 1572872 | tf_op jit(solution)/shard_map/ppermute | solution.py:10
  110.2 17.1 %collective-permute-done.1 = bf16[1024,256]{1,0:T(8,128)(2,1)S(1)} collective-permute-done((bf16[1024,256]{1,0:T(8,128)(2,1)S(1)}, bf16[1024,256]{1,0:T(8,128)(2,1)S(1)}, u32[]{:S(2)}, u32[]{:S(2)}) %collective-permute-start.1) | collective-permute-done | bytes 524320 | tf_op jit(solution)/shard_map/ppermute | solution.py:10
  127.4 0.8 copy-done.4
  128.5 4.3 scatter_custom_fusion.3
  132.8 40.6 %reduce-scatter.5.cloned.1.call-done = bf16[128,256]{1,0:T(8,128)(2,1)} async-done(((bf16[1024,256]{1,0:T(8,128)(2,1)}), bf16[128,256]{1,0:T(8,128)(2,1)}) %reduce-scatter.5.cloned.1.call-update) | async-done | bytes 65552 | tf_op jit(solution)/shard_map/reduce_scatter | solution.py:90
  173.4 1.5 convert_add_fusion
  174.9 574.3 %all-reduce.2.cloned.1.call-done = f32[1024,256]{1,0:T(8,128)} async-done(((f32[1024,256]{1,0:T(8,128)}), f32[1024,256]{1,0:T(8,128)}) %all-reduce.2.cloned.1.call-update) | async-done | bytes 1048592 | tf_op jit(solution)/shard_map/psum | solution.py:84
  749.2 2.3 copy.25
  (42 shorter events, 4.0 us)
Async XLA Ops:
  8.0 30.3 %copy-start = (f32[1024,256]{1,0:T(8,128)S(1)}, f32[1024,256]{1,0:T(8,128)}, u32[]{:S(2)}) copy-start(f32[1024,256]{1,0:T(8,128)} %param.8) | copy-start | bytes 3145732
  8.0 124.8 %reduce-scatter.3.cloned.1.call-start = ((), (), s32[]{:S(2)}) async-start(), calls=%async_computation.2 | async-start | bytes 589824 | tf_op jit(solution)/shard_map/reduce_scatter | solution.py:89
  29.2 30.7 %collective-permute-start = (bf16[1024,256]{1,0:T(8,128)(2,1)S(1)}, bf16[1024,256]{1,0:T(8,128)(2,1)S(1)}, u32[]{:S(2)}, u32[]{:S(2)}) collective-permute-start(bf16[1024,256]{1,0:T(8,128)(2,1)S(1)} %all_gather.3), channel_id=1, source_target_pairs={{256,0},{264,8},{272,16},{280,24},{288,32},{296,40},{304,48},{312,... | collective-permute-start | bytes 1572872 | tf_op jit(solution)/shard_map/ppermute | solution.py:10
  38.3 2.3 copy-start.5
  38.3 3.0 copy-start.6
  71.1 3.0 copy-start.2
  74.0 1.6 copy-start.1
  75.9 6.2 copy-start.3
  81.8 91.6 %reduce-scatter.5.cloned.1.call-start = ((), (), s32[]{:S(2)}) async-start(), calls=%async_computation.3 | async-start | bytes 589824 | tf_op jit(solution)/shard_map/reduce_scatter | solution.py:90
  101.9 25.5 %collective-permute-start.1 = (bf16[1024,256]{1,0:T(8,128)(2,1)S(1)}, bf16[1024,256]{1,0:T(8,128)(2,1)S(1)}, u32[]{:S(2)}, u32[]{:S(2)}) collective-permute-start(bf16[1024,256]{1,0:T(8,128)(2,1)S(1)} %convert_element_type.32), channel_id=1, source_target_pairs={{256,0},{264,8},{272,16},{280,24},{288,32},{296,40},{304,48},{312,... | collective-permute-start | bytes 1572872 | tf_op jit(solution)/shard_map/ppermute | solution.py:10
  127.4 0.8 copy-start.4
  128.2 621.0 %all-reduce.2.cloned.1.call-start = ((), (), s32[]{:S(2)}) async-start(), calls=%async_computation.4 | async-start | bytes 2097152 | tf_op jit(solution)/shard_map/psum | solution.py:84
Sparse Core Ops, SparseCore 0:
  81.9 41.4 reduce-scatter.2
  128.3 45.0 reduce-scatter.4
Sparse Core Ops, SparseCore 1:
  132.9 616.3 all-reduce.1
where the time goes:
time: 759 us
  waiting for transfers between devices  647 us (85%)
  other arithmetic  28.7 us (4%)
  local copies, waits for them, and re-layouts  21.3 us (3%)
  blocking collectives  21.1 us (3%)
  between operations  16.4 us (2%)
  starting transfers between devices  16.3 us (2%)
  matrix products  8.1 us (1%)
    psum x1, waiting for transfers between devices, local(): rel_total = lax.psum(rel_partial, 'dom')  574 us
    reduce_scatter x1, waiting for transfers between devices, local(): lax.psum_scatter(returned, 'rel', scatter_dimension=0, tiled=True)  40.6 us
    ppermute x2, waiting for transfers between devices, from_behind(): return lax.ppermute(block, axis, route)  32.1 us
    all_gather x1, blocking collectives, local(): own_block = lax.all_gather(embeddings, 'rel', axis=0, tiled=True)  21.1 us
    ppermute x2, starting transfers between devices, from_behind(): return lax.ppermute(block, axis, route)  16 us
  transfers between devices with their start and end apart: 5, of which 4 were waited for; matrix products, arithmetic and copies ran while one was open for 4% of the time, Pallas kernels for 0%

commit v1 on v0

v1 whole, which is shorter than its diff:
```python
import jax
import jax.numpy as jnp
from jax import lax
from jax.experimental import pallas as pl
from jax.experimental.pallas import tpu as pltpu
from jax.sharding import Mesh
from jax.sharding import PartitionSpec as P

F32 = jnp.float32
BF16 = jnp.bfloat16
AXES = ("yh", "yl", "x", "zl", "zh", "core")
Y = ("yh", "yl")
XZ = ("x", "zl")

D = 256
HALF = 128
SHARD = 128
EDGES = 512
CHUNK = 256
PARTS = 1024


def dot(a, b, ca, cb):
    return lax.dot_general(a, b, (((ca,), (cb,)), ((), ())), preferred_element_type=F32)


def edge_kernel(
    scal_ref, lhs_ref, rhs_ref, rel_ref, neg_ref, mine_ref, other_ref, table_ref,
    mine_out, other_out, rel_out,
    counts,
):
    live, core = scal_ref[0], scal_ref[1]
    weight = neg_ref.shape[1] ** (-0.5)

    def place(ids):
        owner = jnp.bitwise_and(jnp.right_shift(ids, 7), 1)
        slot = jnp.right_shift(ids, 8)
        side = jnp.where(owner == core, 0, 512)
        return side + slot * SHARD + jnp.bitwise_and(ids, SHARD - 1)

    def chunk_of(ref_a, ref_b, part, step):
        ref = ref_a if step < 2 else ref_b
        s = 2 * (step % 2)
        return jnp.concatenate(
            [ref[s, part * SHARD:(part + 1) * SHARD], ref[s + 1, part * SHARD:(part + 1) * SHARD]], axis=0
        )

    lhs = place(lhs_ref[...])
    rhs = place(rhs_ref[...])
    rel = rel_ref[...]
    neg = place(neg_ref[...])
    alive = (lax.broadcasted_iota(jnp.int32, (1, EDGES), 1) < live).astype(F32)
    rows = lax.broadcasted_iota(jnp.int32, (CHUNK, EDGES), 0)

    def one_hot(ids, step):
        return (rows == ids - step * CHUNK).astype(F32).astype(BF16)

    lane_rows = lax.broadcasted_iota(jnp.int32, (CHUNK, 128), 0)
    for step in range(PARTS // CHUNK):
        total = jnp.zeros((CHUNK, 128), F32)
        for k in range(neg.shape[1] // 128):
            total = total + (lane_rows == neg[:, k * 128:(k + 1) * 128] - step * CHUNK).astype(F32)
        counts[step * CHUNK:(step + 1) * CHUNK, :] = jnp.broadcast_to(
            jnp.sum(total, axis=1, keepdims=True) * weight, (CHUNK, 128)
        )

    w = jnp.zeros((D, EDGES), F32)
    h = jnp.zeros((D, EDGES), F32)
    t = jnp.zeros((D, EDGES), F32)
    for step in range(PARTS // CHUNK):
        table = table_ref[step * CHUNK:(step + 1) * CHUNK, :]
        high = table.astype(BF16)
        low = (table - high.astype(F32)).astype(BF16)
        hot = one_hot(rel, step)
        w = w + dot(high, hot, 0, 0) + dot(low, hot, 0, 0)
        h = h + dot(chunk_of(mine_ref, other_ref, 0, step), one_hot(lhs, step), 0, 0)
        t = t + dot(chunk_of(mine_ref, other_ref, 1, step), one_hot(rhs, step), 0, 0)
    w_re, w_im, h_re, h_im = w[:HALF], w[HALF:], h[:HALF], h[HALF:]
    query = jnp.concatenate([h_re * w_re - h_im * w_im, h_re * w_im + h_im * w_re], axis=0).astype(BF16)
    pos = jnp.sum(query.astype(F32) * t, axis=0, keepdims=True)
    pos_grad = (0.5 * jnp.tanh(0.5 * pos) - 0.5) * alive

    grad = jnp.zeros((D, EDGES), F32)
    for step in range(PARTS // CHUNK):
        tails = chunk_of(mine_ref, other_ref, 1, step)
        scores = dot(tails, query, 1, 0)
        often = counts[step * CHUNK:(step + 1) * CHUNK, :]
        often = jnp.concatenate([often] * (EDGES // 128), axis=1)
        both = (0.5 * jnp.tanh(0.5 * scores) + 0.5) * often * alive
        both = both + jnp.where(rows == rhs - step * CHUNK, pos_grad, 0.0)
        both = both.astype(BF16)
        grad = grad + dot(tails, both, 0, 0)
        out = dot(both, query, 1, 1).astype(BF16)
        ref = mine_out if step < 2 else other_out
        s = 2 * (step % 2)
        ref[s, SHARD:, :] = out[:SHARD]
        ref[s + 1, SHARD:, :] = out[SHARD:]

    g_re, g_im = grad[:HALF], grad[HALF:]
    head = jnp.concatenate([g_re * w_re + g_im * w_im, g_im * w_re - g_re * w_im], axis=0).astype(BF16)
    term = jnp.concatenate([g_re * h_re + g_im * h_im, g_im * h_re - g_re * h_im], axis=0).astype(BF16)
    for step in range(PARTS // CHUNK):
        out = dot(one_hot(lhs, step), head, 1, 1).astype(BF16)
        ref = mine_out if step < 2 else other_out
        s = 2 * (step % 2)
        ref[s, :SHARD, :] = out[:SHARD]
        ref[s + 1, :SHARD, :] = out[SHARD:]
        out = dot(one_hot(rel, step), term, 1, 1).astype(BF16)
        rel_out[2 * step] = out[:SHARD]
        rel_out[2 * step + 1] = out[SHARD:]


def edge_terms(scalars, lhs, rhs, rel, neg, mine, other, table):
    vmem = pl.BlockSpec(memory_space=pltpu.VMEM)
    block = jax.ShapeDtypeStruct((4, 2 * SHARD, D), BF16)
    return pl.pallas_call(
        edge_kernel,
        out_shape=(block, block, jax.ShapeDtypeStruct((8, SHARD, D), BF16)),
        in_specs=[pl.BlockSpec(memory_space=pltpu.SMEM)] + [vmem] * 7,
        out_specs=(vmem, vmem, vmem),
        scratch_shapes=[pltpu.VMEM((PARTS, 128), F32)],
        compiler_params=pltpu.CompilerParams(vmem_limit_bytes=40 << 20),
    )(scalars, lhs, rhs, rel, neg, mine, other, table)


def swap(block, axis, distance=1):
    size = lax.axis_size(axis)
    return lax.ppermute(block, axis, [(i, i ^ distance) for i in range(size)])


def spread(block, axis, size):
    copies = jnp.broadcast_to(block[None], (size,) + block.shape)
    return lax.all_to_all(copies, axis, 0, 0)


def summed(blocks, axis):
    return jnp.sum(lax.all_to_all(blocks, axis, 0, 0).astype(F32), axis=0)


def tie(*values):
    return lax.optimization_barrier(values)


def local(embeddings, relations, lhs_ids, rhs_ids, rel_ids, neg_ids, live):
    zh = lax.axis_index("zh")
    tails = swap(embeddings, "yh")
    mine = spread(jnp.concatenate([embeddings, tails], axis=0), "zh", 4)
    other = swap(mine, "core")
    scalars = jnp.concatenate([live, lax.axis_index("core").astype(jnp.int32)[None]])
    mine_sum, other_sum, rel_part = edge_terms(
        scalars, lhs_ids[0], rhs_ids[0], rel_ids[0], neg_ids[0, 0], mine, other, relations
    )
    from_core = swap(other_sum, "core")
    rel_xz = summed(rel_part, XZ).astype(BF16)
    from_core, rel_xz = tie(from_core, rel_xz)

    chip = (mine_sum.astype(F32) + from_core.astype(F32)).astype(BF16)
    high = zh // 2
    pairs = chip.reshape(2, 2, 2 * SHARD, D)
    keep = lax.dynamic_index_in_dim(pairs, high, 0, keepdims=False)
    from_two = swap(lax.dynamic_index_in_dim(pairs, 1 - high, 0, keepdims=False), "zh", 2)
    rel_y = summed(rel_xz.reshape(8, 16, D), Y).astype(BF16)
    from_two, rel_y = tie(from_two, rel_y)

    quad = (keep.astype(F32) + from_two.astype(F32)).astype(BF16)
    low = zh % 2
    keep = lax.dynamic_index_in_dim(quad, low, 0, keepdims=False)
    from_one = swap(lax.dynamic_index_in_dim(quad, 1 - low, 0, keepdims=False), "zh", 1)
    rel_all_y = spread(rel_y, Y, 8).reshape(SHARD, D)
    from_one, rel_all_y = tie(from_one, rel_all_y)

    shard = keep.astype(F32) + from_one.astype(F32)
    back = swap(shard[SHARD:].astype(BF16), "yh")
    rel_all = spread(rel_all_y, XZ, 8).reshape(PARTS, D)
    return shard[:SHARD] + back.astype(F32), rel_all.astype(F32)


def solution(mesh):
    fine = Mesh(mesh.devices.reshape(2, 4, 4, 2, 4, 2), AXES)
    dom, rel = AXES[:4], AXES[4:]
    placed = (
        P(AXES, None),
        P(rel, None),
        P(dom, rel, None),
        P(dom, rel, None),
        P(dom, rel, None),
        P(dom, rel, None, None),
        P(AXES),
    )
    return jax.shard_map(
        local,
        mesh=fine,
        in_specs=placed,
        out_specs=(P(AXES, None), P(rel, None)),
        check_vma=False,
    )
```

time: 759 us -> 118 us (0.16)
  waiting for transfers between devices: 647 us -> 27.4 us
  other arithmetic: 28.7 us -> 3.62 us
  starting transfers between devices: 16.3 us -> 39.8 us
  local copies, waits for them, and re-layouts: 21.3 us -> 1.62 us
  blocking collectives: 21.1 us -> 37.9 us
  between operations: 16.4 us -> 1.48 us
  matrix products: 8.1 us -> 0 us
    psum x1 -> x0, waiting for transfers between devices: 574 us -> none  [local(): rel_total = lax.psum(rel_partial, 'dom')]
    reduce_scatter x2 -> x0, waiting for transfers between devices: 40.6 us -> none  [the longest x1 40.6 us: local(): lax.psum_scatter(returned, 'rel', scatter_dimension=0, tiled=True)]
    all_to_all x0 -> x2, blocking collectives: none -> 37.9 us  [spread(): return lax.all_to_all(copies, axis, 0, 0)]
    scatter-add x4 -> x0, other arithmetic: 24.3 us -> none  [the longest x1 12.4 us: edge_terms(): partner_grad = partner_grad.at[neg_index[0]].add(row_grad)]
    all_gather x1 -> x0, blocking collectives: 21.1 us -> none  [local(): own_block = lax.all_gather(embeddings, 'rel', axis=0, tiled=True)]
    ppermute x2 -> x6, waiting for transfers between devices: 32.1 us -> 12.6 us  [swap(): return lax.ppermute(block, axis, [(i, i ^ distance) for i in range(size)])]
    all_to_all x0 -> x3, starting transfers between devices: none -> 17.7 us  [the longest x2 11.9 us: summed(): return jnp.sum(lax.all_to_all(blocks, axis, 0, 0).astype(F32), axis=0)]
    gather x6 -> x0, local copies, waits for them, and re-layouts: 14.8 us -> none  [the longest x1 9.05 us: edge_terms(): neg_rows = partner_block[neg_index[0]]]
  transfers between devices with their start and end apart: 5 -> 9, of which waited for: 4 -> 5; matrix products, arithmetic and copies ran while one was open for 4% -> 1% of each run, Pallas kernels for 0% -> 0%
where the time goes in v1:
time: 118 us; the launch traced here: 117 us
  starting transfers between devices  39.8 us (34%)
  blocking collectives  37.9 us (32%)
  waiting for transfers between devices  27.4 us (23%)
  Pallas kernels  5.5 us (5%)
  other arithmetic  3.62 us (3%)
  local copies, waits for them, and re-layouts  1.62 us (1%)
  between operations  1.48 us (1%)
    all_to_all x2, blocking collectives, spread(): return lax.all_to_all(copies, axis, 0, 0)  37.9 us
    ppermute x6, starting transfers between devices, swap(): return lax.ppermute(block, axis, [(i, i ^ distance) for i in range(size)])  22.1 us
    all_to_all x2, waiting for transfers between devices, summed(): return jnp.sum(lax.all_to_all(blocks, axis, 0, 0).astype(F32), axis=0)  14.8 us
    ppermute x6, waiting for transfers between devices, swap(): return lax.ppermute(block, axis, [(i, i ^ distance) for i in range(size)])  12.6 us
    all_to_all x2, starting transfers between devices, summed(): return jnp.sum(lax.all_to_all(blocks, axis, 0, 0).astype(F32), axis=0)  11.9 us
    all_to_all x1, starting transfers between devices, spread(): return lax.all_to_all(copies, axis, 0, 0)  5.81 us
    pallas_call x1, Pallas kernels, edge_terms(): pl.pallas_call(edge_kernel, out_shape=(block, block, jax.ShapeDtypeStruct...  5.5 us
  transfers between devices with their start and end apart: 9, of which 5 were waited for; matrix products, arithmetic and copies ran while one was open for 1% of the time, Pallas kernels for 0%

profile of v1, /device:TPU:2, one launch (start us, length us, event | category | flops | bytes accessed | tf_op | source)
XLA Modules:
  0.0 117.3 jit_solution(16379915337508839463)
XLA Ops:
  0.6 7.9 %collective-permute-start = (bf16[128,256]{1,0:T(8,128)(2,1)}, bf16[128,256]{1,0:T(8,128)(2,1)S(1)}, u32[]{:S(2)}, u32[]{:S(2)}) collective-permute-start(bf16[128,256]{1,0:T(8,128)(2,1)} %param.7), channel_id=1, source_target_pairs={{0,256},{256,0},{1,257},{257,1},{2,258},{258,2},{3,259},{259,3},{4... | collective-permute-start | bytes 196616 | tf_op jit(solution)/shard_map/ppermute | solution.py:128
  8.5 3.3 %collective-permute-done = bf16[128,256]{1,0:T(8,128)(2,1)S(1)} collective-permute-done((bf16[128,256]{1,0:T(8,128)(2,1)}, bf16[128,256]{1,0:T(8,128)(2,1)S(1)}, u32[]{:S(2)}, u32[]{:S(2)}) %collective-permute-start) | collective-permute-done | bytes 65568 | tf_op jit(solution)/shard_map/ppermute | solution.py:128
  11.8 0.8 pad_maximum_fusion
  12.7 25.6 %all_to_all.25.mine_ref = bf16[4,256,256]{2,1,0:T(8,128)(2,1)S(1)} all-to-all(bf16[4,256,256]{2,1,0:T(8,128)(2,1)S(1)} %broadcast_in_dim.9), channel_id=1, replica_groups=mesh['yh'=2,'yl'=4,'x'=4,'zl'=2,'zh'=4,'core'=2] {'zh'}, dimensions={0} | all-to-all | bytes 1048576 | tf_op jit(solution)/shard_map/all_to_all | solution.py:133
  38.3 1.9 %collective-permute-start.1 = (bf16[4,256,256]{2,1,0:T(8,128)(2,1)S(1)}, bf16[4,256,256]{2,1,0:T(8,128)(2,1)S(1)}, u32[]{:S(2)}, u32[]{:S(2)}) collective-permute-start(bf16[4,256,256]{2,1,0:T(8,128)(2,1)S(1)} %all_to_all.25.mine_ref), channel_id=1, source_target_pairs={{0,1},{1,0},{2,3},{3,2},{4,5},{5,4},{6,7},{7,6},{8,9},{9,8},{10,11... | collective-permute-start | bytes 1572872 | tf_op jit(solution)/shard_map/ppermute | solution.py:128
  40.9 1.1 collective-permute-done.1.other_ref
  42.1 0.7 copy-done.3
  42.7 5.5 %shard_map.86 = (bf16[4,256,256]{2,1,0:T(8,128)(2,1)S(1)}, bf16[4,256,256]{2,1,0:T(8,128)(2,1)S(1)}, bf16[8,128,256]{2,1,0:T(8,128)(2,1)}) custom-call(s32[2]{0:T(128)S(1)} %pad_add_fusion.scal_ref, s32[1,512]{1,0:T(1,128)S(1)} %bitcast.22, s32[1,512]{1,0:T(1,128)S(1)} %bitcast.23, s32[1,512]{1,0:T(1,128)S(1)} %bitcast.24, s32[1,2048]{1,0:T(1,128)S(1)} %bitcast.21, ...), custom_call_target="tpu_custom_call" | custom-call | tf_op jit(solution)/shard_map/pallas_call | solution.py:116
  48.3 4.8 %all-to-all-start.1 = ((bf16[8,128,256]{2,1,0:T(8,128)(2,1)}), bf16[8,128,256]{2,1,0:T(8,128)(2,1)S(1)}, u32[]{:S(2)}, u32[]{:S(2)}) async-start(bf16[8,128,256]{2,1,0:T(8,128)(2,1)} %get-tuple-element.13), calls=%async_computation.1 | async-start | bytes 1048576 | tf_op jit(solution)/shard_map/all_to_all | solution.py:137
  53.1 1.9 %collective-permute-start.2 = (bf16[4,256,256]{2,1,0:T(8,128)(2,1)S(1)}, bf16[4,256,256]{2,1,0:T(8,128)(2,1)S(1)}, u32[]{:S(2)}, u32[]{:S(2)}) collective-permute-start(bf16[4,256,256]{2,1,0:T(8,128)(2,1)S(1)} %get-tuple-element.12), channel_id=1, source_target_pairs={{0,1},{1,0},{2,3},{3,2},{4,5},{5,4},{6,7},{7,6},{8,9},{9,8},{10,11... | collective-permute-start | bytes 1572872 | tf_op jit(solution)/shard_map/ppermute | solution.py:128
  55.0 6.4 %all-to-all-done.1 = bf16[8,128,256]{2,1,0:T(8,128)(2,1)S(1)} async-done(((bf16[8,128,256]{2,1,0:T(8,128)(2,1)}), bf16[8,128,256]{2,1,0:T(8,128)(2,1)S(1)}, u32[]{:S(2)}, u32[]{:S(2)}) %all-to-all-start.1) | async-done | bytes 524320 | tf_op jit(solution)/shard_map/all_to_all | solution.py:137
  61.4 0.7 reduce_sum.24
  62.1 0.1 add_convert_fusion
  62.3 3.8 %collective-permute-start.3 = (bf16[2,256,256]{2,1,0:T(8,128)(2,1)S(1)}, bf16[2,256,256]{2,1,0:T(8,128)(2,1)S(1)}, u32[]{:S(2)}, u32[]{:S(2)}) collective-permute-start(bf16[2,256,256]{2,1,0:T(8,128)(2,1)S(1)} %dynamic-slice_bitcast_fusion), channel_id=1, source_target_pairs={{0,4},{2,6},{4,0},{6,2},{1,5},{3,7},{5,1},{7,3},{8,12},{10,14},{12... | collective-permute-start | bytes 786440 | tf_op jit(solution)/shard_map/ppermute | solution.py:128
  66.1 7.1 %all-to-all-start.2 = ((bf16[8,16,256]{2,1,0:T(8,128)(2,1)}), bf16[8,16,256]{2,1,0:T(8,128)(2,1)S(1)}, u32[]{:S(2)}, u32[]{:S(2)}) async-start(bf16[8,16,256]{2,1,0:T(8,128)(2,1)} %bitcast.8), calls=%async_computation.2 | async-start | bytes 131072 | tf_op jit(solution)/shard_map/all_to_all | solution.py:137
  73.2 8.4 %all-to-all-done.2 = bf16[8,16,256]{2,1,0:T(8,128)(2,1)S(1)} async-done(((bf16[8,16,256]{2,1,0:T(8,128)(2,1)}), bf16[8,16,256]{2,1,0:T(8,128)(2,1)S(1)}, u32[]{:S(2)}, u32[]{:S(2)}) %all-to-all-start.2) | async-done | bytes 65568 | tf_op jit(solution)/shard_map/all_to_all | solution.py:137
  81.7 4.3 %collective-permute-start.4 = (bf16[256,256]{1,0:T(8,128)(2,1)S(1)}, bf16[256,256]{1,0:T(8,128)(2,1)S(1)}, u32[]{:S(2)}, u32[]{:S(2)}) collective-permute-start(bf16[256,256]{1,0:T(8,128)(2,1)S(1)} %dynamic-slice_bitcast_fusion.1), channel_id=1, source_target_pairs={{0,2},{2,0},{4,6},{6,4},{1,3},{3,1},{5,7},{7,5},{8,10},{10,8},{12,... | collective-permute-start | bytes 393224 | tf_op jit(solution)/shard_map/ppermute | solution.py:128
  85.9 12.3 %all_to_all.26 = bf16[8,16,256]{2,1,0:T(8,128)(2,1)S(1)} all-to-all(bf16[8,16,256]{2,1,0:T(8,128)(2,1)S(1)} %broadcast_in_dim.10), channel_id=1, replica_groups=mesh['yh'=2,'yl'=4,'x'=4,'zl'=2,'zh'=4,'core'=2] {'yh','yl'}, dimensions={0} | all-to-all | bytes 131072 | tf_op jit(solution)/shard_map/all_to_all | solution.py:133
  98.2 0.8 broadcast_in_dim.11
  99.1 5.8 %all-to-all-start.4 = ((bf16[8,128,256]{2,1,0:T(8,128)(2,1)}), bf16[8,128,256]{2,1,0:T(8,128)(2,1)S(1)}, u32[]{:S(2)}, u32[]{:S(2)}) async-start(bf16[8,128,256]{2,1,0:T(8,128)(2,1)} %broadcast_in_dim.11), calls=%async_computation.4 | async-start | bytes 1048576 | tf_op jit(solution)/shard_map/all_to_all | solution.py:133
  104.9 2.4 %collective-permute-start.5 = (bf16[128,256]{1,0:T(8,128)(2,1)S(1)}, bf16[128,256]{1,0:T(8,128)(2,1)S(1)}, u32[]{:S(2)}, u32[]{:S(2)}) collective-permute-start(bf16[128,256]{1,0:T(8,128)(2,1)S(1)} %slice.13), channel_id=1, source_target_pairs={{0,256},{256,0},{1,257},{257,1},{2,258},{258,2},{3,259},{259,3},{4... | collective-permute-start | bytes 196616 | tf_op jit(solution)/shard_map/ppermute | solution.py:128
  107.3 8.2 %collective-permute-done.5 = bf16[128,256]{1,0:T(8,128)(2,1)S(1)} collective-permute-done((bf16[128,256]{1,0:T(8,128)(2,1)S(1)}, bf16[128,256]{1,0:T(8,128)(2,1)S(1)}, u32[]{:S(2)}, u32[]{:S(2)}) %collective-permute-start.5) | collective-permute-done | bytes 65568 | tf_op jit(solution)/shard_map/ppermute | solution.py:128
  115.6 0.7 slice_add_fusion
  116.2 1.1 bitcast_convert_fusion
  (22 shorter events, 0.3 us)
Async XLA Ops:
  0.6 41.4 %copy-start = (f32[1024,256]{1,0:T(8,128)S(1)}, f32[1024,256]{1,0:T(8,128)}, u32[]{:S(2)}) copy-start(f32[1024,256]{1,0:T(8,128)} %table_ref.1) | copy-start | bytes 3145732
  0.6 11.1 %collective-permute-start = (bf16[128,256]{1,0:T(8,128)(2,1)}, bf16[128,256]{1,0:T(8,128)(2,1)S(1)}, u32[]{:S(2)}, u32[]{:S(2)}) collective-permute-start(bf16[128,256]{1,0:T(8,128)(2,1)} %param.7), channel_id=1, source_target_pairs={{0,256},{256,0},{1,257},{257,1},{2,258},{258,2},{3,259},{259,3},{4... | collective-permute-start | bytes 196616 | tf_op jit(solution)/shard_map/ppermute | solution.py:128
  12.7 29.4 %copy-start.4 = (s32[1,1,512]{2,1,0:T(1,128)S(1)}, s32[1,1,512]{2,1,0:T(1,128)}, u32[]{:S(2)}) copy-start(s32[1,1,512]{2,1,0:T(1,128)} %param.11) | copy-start | bytes 6148
  38.3 3.8 %collective-permute-start.1 = (bf16[4,256,256]{2,1,0:T(8,128)(2,1)S(1)}, bf16[4,256,256]{2,1,0:T(8,128)(2,1)S(1)}, u32[]{:S(2)}, u32[]{:S(2)}) collective-permute-start(bf16[4,256,256]{2,1,0:T(8,128)(2,1)S(1)} %all_to_all.25.mine_ref), channel_id=1, source_target_pairs={{0,1},{1,0},{2,3},{3,2},{4,5},{5,4},{6,7},{7,6},{8,9},{9,8},{10,11... | collective-permute-start | bytes 1572872 | tf_op jit(solution)/shard_map/ppermute | solution.py:128
  40.2 1.9 %copy-start.1 = (s32[1,1,1,2048]{3,2,1,0:T(1,128)S(1)}, s32[1,1,1,2048]{3,2,1,0:T(1,128)}, u32[]{:S(2)}) copy-start(s32[1,1,1,2048]{3,2,1,0:T(1,128)} %param.12) | copy-start | bytes 24580
  42.1 0.7 copy-start.3
  42.1 0.7 copy-start.2
  48.3 13.2 %all-to-all-start.1 = ((bf16[8,128,256]{2,1,0:T(8,128)(2,1)}), bf16[8,128,256]{2,1,0:T(8,128)(2,1)S(1)}, u32[]{:S(2)}, u32[]{:S(2)}) async-start(bf16[8,128,256]{2,1,0:T(8,128)(2,1)} %get-tuple-element.13), calls=%async_computation.1 | async-start | bytes 1048576 | tf_op jit(solution)/shard_map/all_to_all | solution.py:137
  53.1 9.0 %collective-permute-start.2 = (bf16[4,256,256]{2,1,0:T(8,128)(2,1)S(1)}, bf16[4,256,256]{2,1,0:T(8,128)(2,1)S(1)}, u32[]{:S(2)}, u32[]{:S(2)}) collective-permute-start(bf16[4,256,256]{2,1,0:T(8,128)(2,1)S(1)} %get-tuple-element.12), channel_id=1, source_target_pairs={{0,1},{1,0},{2,3},{3,2},{4,5},{5,4},{6,7},{7,6},{8,9},{9,8},{10,11... | collective-permute-start | bytes 1572872 | tf_op jit(solution)/shard_map/ppermute | solution.py:128
  62.3 19.3 %collective-permute-start.3 = (bf16[2,256,256]{2,1,0:T(8,128)(2,1)S(1)}, bf16[2,256,256]{2,1,0:T(8,128)(2,1)S(1)}, u32[]{:S(2)}, u32[]{:S(2)}) collective-permute-start(bf16[2,256,256]{2,1,0:T(8,128)(2,1)S(1)} %dynamic-slice_bitcast_fusion), channel_id=1, source_target_pairs={{0,4},{2,6},{4,0},{6,2},{1,5},{3,7},{5,1},{7,3},{8,12},{10,14},{12... | collective-permute-start | bytes 786440 | tf_op jit(solution)/shard_map/ppermute | solution.py:128
  66.1 15.5 %all-to-all-start.2 = ((bf16[8,16,256]{2,1,0:T(8,128)(2,1)}), bf16[8,16,256]{2,1,0:T(8,128)(2,1)S(1)}, u32[]{:S(2)}, u32[]{:S(2)}) async-start(bf16[8,16,256]{2,1,0:T(8,128)(2,1)} %bitcast.8), calls=%async_computation.2 | async-start | bytes 131072 | tf_op jit(solution)/shard_map/all_to_all | solution.py:137
  81.7 16.6 %collective-permute-start.4 = (bf16[256,256]{1,0:T(8,128)(2,1)S(1)}, bf16[256,256]{1,0:T(8,128)(2,1)S(1)}, u32[]{:S(2)}, u32[]{:S(2)}) collective-permute-start(bf16[256,256]{1,0:T(8,128)(2,1)S(1)} %dynamic-slice_bitcast_fusion.1), channel_id=1, source_target_pairs={{0,2},{2,0},{4,6},{6,4},{1,3},{3,1},{5,7},{7,5},{8,10},{10,8},{12,... | collective-permute-start | bytes 393224 | tf_op jit(solution)/shard_map/ppermute | solution.py:128
  99.1 17.1 %all-to-all-start.4 = ((bf16[8,128,256]{2,1,0:T(8,128)(2,1)}), bf16[8,128,256]{2,1,0:T(8,128)(2,1)S(1)}, u32[]{:S(2)}, u32[]{:S(2)}) async-start(bf16[8,128,256]{2,1,0:T(8,128)(2,1)} %broadcast_in_dim.11), calls=%async_computation.4 | async-start | bytes 1048576 | tf_op jit(solution)/shard_map/all_to_all | solution.py:133
  104.9 10.6 %collective-permute-start.5 = (bf16[128,256]{1,0:T(8,128)(2,1)S(1)}, bf16[128,256]{1,0:T(8,128)(2,1)S(1)}, u32[]{:S(2)}, u32[]{:S(2)}) collective-permute-start(bf16[128,256]{1,0:T(8,128)(2,1)S(1)} %slice.13), channel_id=1, source_target_pairs={{0,256},{256,0},{1,257},{257,1},{2,258},{258,2},{3,259},{259,3},{4... | collective-permute-start | bytes 196616 | tf_op jit(solution)/shard_map/ppermute | solution.py:128

commit v2 on v1

v2 whole, which is shorter than its diff:
```python
import jax
import jax.numpy as jnp
from jax import lax
from jax.experimental import pallas as pl
from jax.experimental.pallas import tpu as pltpu
from jax.sharding import Mesh
from jax.sharding import PartitionSpec as P

F32 = jnp.float32
BF16 = jnp.bfloat16
AXES = ("yh", "yl", "x", "zl", "zh", "core")
Y = ("yh", "yl")
XZ = ("x", "zl")

D = 256
HALF = 128
SHARD = 128
EDGES = 512
CHUNK = 256
PARTS = 1024


def dot(a, b, ca, cb):
    return lax.dot_general(a, b, (((ca,), (cb,)), ((), ())), preferred_element_type=F32)


def place(ids, core):
    owner = jnp.bitwise_and(jnp.right_shift(ids, 7), 1)
    side = jnp.where(owner == core, 0, 512)
    return side + jnp.right_shift(ids, 8) * SHARD + jnp.bitwise_and(ids, SHARD - 1)


def one_hot(ids, step):
    rows = lax.broadcasted_iota(jnp.int32, (CHUNK, EDGES), 0)
    return (rows == ids - step * CHUNK).astype(F32).astype(BF16)


def early_kernel(scal_ref, rel_ref, neg_ref, table_ref, w_out, counts_out):
    weight = neg_ref.shape[1] ** (-0.5)
    neg = place(neg_ref[...], scal_ref[1])
    rel = rel_ref[...]
    lane_rows = lax.broadcasted_iota(jnp.int32, (CHUNK, 128), 0)
    w = jnp.zeros((D, EDGES), F32)
    for step in range(PARTS // CHUNK):
        table = table_ref[step * CHUNK:(step + 1) * CHUNK, :]
        high = table.astype(BF16)
        low = (table - high.astype(F32)).astype(BF16)
        hot = one_hot(rel, step)
        w = w + dot(high, hot, 0, 0) + dot(low, hot, 0, 0)
        total = jnp.zeros((CHUNK, 128), F32)
        for k in range(neg.shape[1] // 128):
            total = total + (lane_rows == neg[:, k * 128:(k + 1) * 128] - step * CHUNK).astype(F32)
        counts_out[step * CHUNK:(step + 1) * CHUNK, :] = jnp.broadcast_to(
            jnp.sum(total, axis=1, keepdims=True) * weight, (CHUNK, 128)
        )
    w_out[...] = w


def edge_kernel(
    scal_ref, lhs_ref, rhs_ref, rel_ref, w_ref, counts_ref, mine_ref, other_ref,
    mine_out, other_out, rel_out,
):
    live, core = scal_ref[0], scal_ref[1]

    def chunk_of(part, step):
        ref = mine_ref if step < 2 else other_ref
        s = 2 * (step % 2)
        rows = slice(part * SHARD, (part + 1) * SHARD)
        return jnp.concatenate([ref[s, rows], ref[s + 1, rows]], axis=0)

    def store(part, step, out):
        ref = mine_out if step < 2 else other_out
        s = 2 * (step % 2)
        rows = slice(part * SHARD, (part + 1) * SHARD)
        ref[s, rows, :] = out[:SHARD]
        ref[s + 1, rows, :] = out[SHARD:]

    lhs = place(lhs_ref[...], core)
    rhs = place(rhs_ref[...], core)
    rel = rel_ref[...]
    alive = (lax.broadcasted_iota(jnp.int32, (1, EDGES), 1) < live).astype(F32)
    rows = lax.broadcasted_iota(jnp.int32, (CHUNK, EDGES), 0)

    h = jnp.zeros((D, EDGES), F32)
    t = jnp.zeros((D, EDGES), F32)
    for step in range(PARTS // CHUNK):
        h = h + dot(chunk_of(0, step), one_hot(lhs, step), 0, 0)
        t = t + dot(chunk_of(1, step), one_hot(rhs, step), 0, 0)
    w_re, w_im, h_re, h_im = w_ref[:HALF], w_ref[HALF:], h[:HALF], h[HALF:]
    query = jnp.concatenate([h_re * w_re - h_im * w_im, h_re * w_im + h_im * w_re], axis=0).astype(BF16)
    pos = jnp.sum(query.astype(F32) * t, axis=0, keepdims=True)
    pos_grad = (0.5 * jnp.tanh(0.5 * pos) - 0.5) * alive

    grad = jnp.zeros((D, EDGES), F32)
    for step in range(PARTS // CHUNK):
        tails = chunk_of(1, step)
        scores = dot(tails, query, 1, 0)
        often = counts_ref[step * CHUNK:(step + 1) * CHUNK, :]
        often = jnp.concatenate([often] * (EDGES // 128), axis=1)
        both = (0.5 * jnp.tanh(0.5 * scores) + 0.5) * often * alive
        both = both + jnp.where(rows == rhs - step * CHUNK, pos_grad, 0.0)
        both = both.astype(BF16)
        grad = grad + dot(tails, both, 0, 0)
        store(1, step, dot(both, query, 1, 1).astype(BF16))

    g_re, g_im = grad[:HALF], grad[HALF:]
    term = jnp.concatenate([g_re * h_re + g_im * h_im, g_im * h_re - g_re * h_im], axis=0).astype(BF16)
    head = jnp.concatenate([g_re * w_re + g_im * w_im, g_im * w_re - g_re * w_im], axis=0).astype(BF16)
    for step in range(PARTS // CHUNK):
        out = dot(one_hot(rel, step), term, 1, 1).astype(BF16)
        rel_out[2 * step] = out[:SHARD]
        rel_out[2 * step + 1] = out[SHARD:]
        store(0, step, dot(one_hot(lhs, step), head, 1, 1).astype(BF16))


def early_terms(scalars, rel, neg, table):
    vmem = pl.BlockSpec(memory_space=pltpu.VMEM)
    return pl.pallas_call(
        early_kernel,
        out_shape=(jax.ShapeDtypeStruct((D, EDGES), F32), jax.ShapeDtypeStruct((PARTS, 128), F32)),
        in_specs=[pl.BlockSpec(memory_space=pltpu.SMEM)] + [vmem] * 3,
        out_specs=(vmem, vmem),
        compiler_params=pltpu.CompilerParams(vmem_limit_bytes=24 << 20),
        cost_estimate=pl.CostEstimate(flops=1 << 30, bytes_accessed=3 << 20, transcendentals=0),
    )(scalars, rel, neg, table)


def edge_terms(scalars, lhs, rhs, rel, w, counts, mine, other):
    vmem = pl.BlockSpec(memory_space=pltpu.VMEM)
    block = jax.ShapeDtypeStruct((4, 2 * SHARD, D), BF16)
    return pl.pallas_call(
        edge_kernel,
        out_shape=(block, block, jax.ShapeDtypeStruct((8, SHARD, D), BF16)),
        in_specs=[pl.BlockSpec(memory_space=pltpu.SMEM)] + [vmem] * 7,
        out_specs=(vmem, vmem, vmem),
        compiler_params=pltpu.CompilerParams(vmem_limit_bytes=40 << 20),
    )(scalars, lhs, rhs, rel, w, counts, mine, other)


def swap(block, axis, distance=1):
    size = lax.axis_size(axis)
    return lax.ppermute(block, axis, [(i, i ^ distance) for i in range(size)])


def spread(block, axis, size):
    copies = jnp.broadcast_to(block[None], (size,) + block.shape)
    return lax.all_to_all(copies, axis, 0, 0)


def summed(blocks):
    return jnp.sum(blocks.astype(F32), axis=0).astype(BF16)


def exchange(blocks, axis):
    return lax.all_to_all(blocks, axis, 0, 0)


def tie(*values):
    return lax.optimization_barrier(values)


def local(embeddings, relations, lhs_ids, rhs_ids, rel_ids, neg_ids, live):
    zh = lax.axis_index("zh")
    scalars = jnp.concatenate([live, lax.axis_index("core").astype(jnp.int32)[None]])
    tails = swap(embeddings, "yh")
    w, counts = early_terms(scalars, rel_ids[0], neg_ids[0, 0], relations)
    tails, w, counts = tie(tails, w, counts)
    both = jnp.concatenate([embeddings, tails], axis=0)
    mine = lax.all_gather(both, "zh", axis=0, tiled=False)
    other = swap(mine, "core")
    mine_sum, other_sum, rel_part = edge_terms(
        scalars, lhs_ids[0], rhs_ids[0], rel_ids[0], w, counts, mine, other
    )
    from_core = swap(other_sum, "core")
    parts = exchange(rel_part, XZ)
    from_core, parts = tie(from_core, parts)

    chip = (mine_sum.astype(F32) + from_core.astype(F32)).astype(BF16)
    keep = lax.dynamic_index_in_dim(chip, zh, 0, keepdims=False)
    arrived = []
    for step in (1, 3, 2):
        block = lax.dynamic_index_in_dim(chip, (zh + step) % 4, 0, keepdims=False)
        arrived.append(lax.ppermute(block, "zh", [(i, (i + step) % 4) for i in range(4)]))
    parts = spread(summed(parts), Y, 8)
    *arrived, parts = tie(*arrived, parts)

    shard = keep.astype(F32)
    for block in arrived:
        shard = shard + block.astype(F32)
    back = swap(shard[SHARD:].astype(BF16), "yh")
    rel_all = spread(summed(parts), XZ, 8).reshape(PARTS, D)
    return shard[:SHARD] + back.astype(F32), rel_all.astype(F32)


def solution(mesh):
    fine = Mesh(mesh.devices.reshape(2, 4, 4, 2, 4, 2), AXES)
    dom, rel = AXES[:4], AXES[4:]
    placed = (
        P(AXES, None),
        P(rel, None),
        P(dom, rel, None),
        P(dom, rel, None),
        P(dom, rel, None),
        P(dom, rel, None, None),
        P(AXES),
    )
    return jax.shard_map(
        local,
        mesh=fine,
        in_specs=placed,
        out_specs=(P(AXES, None), P(rel, None)),
        check_vma=False,
    )
```

time: 118 us -> 105 us (0.89)
  the two profiles are of different devices: /device:TPU:2 before, /device:TPU:18 now
where the time goes in v2:
time: 105 us; the launch traced here: 104 us
  starting transfers between devices  49 us (47%)
  blocking collectives  21.8 us (21%)
  waiting for transfers between devices  19.4 us (18%)
  Pallas kernels  6.68 us (6%)
  local copies, waits for them, and re-layouts  3.62 us (3%)
  other arithmetic  2.17 us (2%)
  between operations  1.41 us (1%)
    all_gather x1, blocking collectives, local(): mine = lax.all_gather(both, 'zh', axis=0, tiled=False)  21.8 us
    ppermute x4, starting transfers between devices, swap(): return lax.ppermute(block, axis, [(i, i ^ distance) for i in range(size)])  15.4 us
    all_to_all x2, starting transfers between devices, spread(): return lax.all_to_all(copies, axis, 0, 0)  14.8 us
    ppermute x3, starting transfers between devices, local(): lax.ppermute(block, 'zh', [(i, (i + step) % 4) for i in range(4)])  13 us
    ppermute x4, waiting for transfers between devices, swap(): return lax.ppermute(block, axis, [(i, i ^ distance) for i in range(size)])  9.12 us
    all_to_all x1, starting transfers between devices, exchange(): return lax.all_to_all(blocks, axis, 0, 0)  5.84 us
    ppermute x3, waiting for transfers between devices, local(): lax.ppermute(block, 'zh', [(i, (i + step) % 4) for i in range(4)])  5.75 us
    all_to_all x1, waiting for transfers between devices, exchange(): return lax.all_to_all(blocks, axis, 0, 0)  4.53 us
  transfers between devices with their start and end apart: 10, of which 6 were waited for; matrix products, arithmetic and copies ran while one was open for 1% of the time, Pallas kernels for 2%

profile of v2, /device:TPU:18, one launch (start us, length us, event | category | flops | bytes accessed | tf_op | source)
XLA Modules:
  0.0 104.1 jit_solution(3038493980306074378)
XLA Ops:
  0.6 5.9 %collective-permute-start = (bf16[128,256]{1,0:T(8,128)(2,1)}, bf16[128,256]{1,0:T(8,128)(2,1)S(1)}, u32[]{:S(2)}, u32[]{:S(2)}) collective-permute-start(bf16[128,256]{1,0:T(8,128)(2,1)} %param.7), channel_id=1, source_target_pairs={{0,256},{256,0},{1,257},{257,1},{2,258},{258,2},{3,259},{259,3},{4... | collective-permute-start | bytes 196616 | tf_op jit(solution)/shard_map/ppermute | solution.py:142
  7.3 0.7 copy-done.2
  8.0 1.2 %copy-done.3 = f32[1024,256]{1,0:T(8,128)S(1)} copy-done((f32[1024,256]{1,0:T(8,128)S(1)}, f32[1024,256]{1,0:T(8,128)}, u32[]{:S(2)}) %copy-start.3) | copy-done | bytes 1048600
  9.2 2.5 %shard_map.86 = (f32[256,512]{1,0:T(8,128)S(1)}, f32[1024,128]{1,0:T(8,128)S(1)}) custom-call(s32[2]{0:T(128)S(1)} %pad_add_fusion.scal_ref, s32[1,512]{1,0:T(1,128)S(1)} %bitcast.22, s32[1,2048]{1,0:T(1,128)S(1)} %bitcast.24, f32[1024,256]{1,0:T(8,128)S(1)} %copy-done.3), custom_call_target="tpu_custom_call" | custom-call | flops 1073741824 | bytes 3145728 | tf_op jit(solution)/shard_map/pallas_call | solution.py:118
  12.0 21.8 %all-gather = bf16[1024,256]{1,0:T(8,128)(2,1)S(1)} all-gather(bf16[256,256]{1,0:T(8,128)(2,1)S(1)} %pad_maximum_fusion), channel_id=2, replica_groups=mesh['yh'=2,'yl'=4,'x'=4,'zl'=2,'zh'=4,'core'=2] {'zh'}, dimensions={0}, use_global_device_ids=true | all-gather | bytes 655360 | tf_op jit(solution)/shard_map/all_gather | solution.py:169
  33.7 2.0 %collective-permute-start.1 = (bf16[4,256,256]{2,1,0:T(8,128)(2,1)S(1)}, bf16[4,256,256]{2,1,0:T(8,128)(2,1)S(1)}, u32[]{:S(2)}, u32[]{:S(2)}) collective-permute-start(bf16[4,256,256]{2,1,0:T(8,128)(2,1)S(1)} %bitcast.18), channel_id=1, source_target_pairs={{0,1},{1,0},{2,3},{3,2},{4,5},{5,4},{6,7},{7,6},{8,9},{9,8},{10,11... | collective-permute-start | bytes 1572872 | tf_op jit(solution)/shard_map/ppermute | solution.py:142
  35.8 1.9 %collective-permute-done.1.other_ref = bf16[4,256,256]{2,1,0:T(8,128)(2,1)S(1)} collective-permute-done((bf16[4,256,256]{2,1,0:T(8,128)(2,1)S(1)}, bf16[4,256,256]{2,1,0:T(8,128)(2,1)S(1)}, u32[]{:S(2)}, u32[]{:S(2)}) %collective-permute-start.1) | collective-permute-done | bytes 524320 | tf_op jit(solution)/shard_map/ppermute | solution.py:142
  37.7 4.2 %shard_map.87 = (bf16[4,256,256]{2,1,0:T(8,128)(2,1)S(1)}, bf16[4,256,256]{2,1,0:T(8,128)(2,1)S(1)}, bf16[8,128,256]{2,1,0:T(8,128)(2,1)}) custom-call(s32[2]{0:T(128)S(1)} %pad_add_fusion.scal_ref, s32[1,512]{1,0:T(1,128)S(1)} %bitcast.20, s32[1,512]{1,0:T(1,128)S(1)} %bitcast.21, s32[1,512]{1,0:T(1,128)S(1)} %bitcast.23, ...), custom_call_target="tpu_custom_call" | custom-call | tf_op jit(solution)/shard_map/pallas_call | solution.py:131
  41.9 5.8 %all-to-all-start = ((bf16[8,128,256]{2,1,0:T(8,128)(2,1)}), bf16[8,128,256]{2,1,0:T(8,128)(2,1)S(1)}, u32[]{:S(2)}, u32[]{:S(2)}) async-start(bf16[8,128,256]{2,1,0:T(8,128)(2,1)} %get-tuple-element.23), calls=%async_computation | async-start | bytes 1048576 | tf_op jit(solution)/shard_map/all_to_all | solution.py:155
  47.7 1.9 %collective-permute-start.2 = (bf16[4,256,256]{2,1,0:T(8,128)(2,1)S(1)}, bf16[4,256,256]{2,1,0:T(8,128)(2,1)S(1)}, u32[]{:S(2)}, u32[]{:S(2)}) collective-permute-start(bf16[4,256,256]{2,1,0:T(8,128)(2,1)S(1)} %get-tuple-element.22), channel_id=1, source_target_pairs={{0,1},{1,0},{2,3},{3,2},{4,5},{5,4},{6,7},{7,6},{8,9},{9,8},{10,11... | collective-permute-start | bytes 1572872 | tf_op jit(solution)/shard_map/ppermute | solution.py:142
  49.6 1.9 %collective-permute-done.2 = bf16[4,256,256]{2,1,0:T(8,128)(2,1)S(1)} collective-permute-done((bf16[4,256,256]{2,1,0:T(8,128)(2,1)S(1)}, bf16[4,256,256]{2,1,0:T(8,128)(2,1)S(1)}, u32[]{:S(2)}, u32[]{:S(2)}) %collective-permute-start.2) | collective-permute-done | bytes 524320 | tf_op jit(solution)/shard_map/ppermute | solution.py:142
  51.5 4.5 %all-to-all-done = bf16[8,128,256]{2,1,0:T(8,128)(2,1)S(1)} async-done(((bf16[8,128,256]{2,1,0:T(8,128)(2,1)}), bf16[8,128,256]{2,1,0:T(8,128)(2,1)S(1)}, u32[]{:S(2)}, u32[]{:S(2)}) %all-to-all-start) | async-done | bytes 524320 | tf_op jit(solution)/shard_map/all_to_all | solution.py:155
  56.1 0.8 broadcast_in_dim.7
  56.9 8.3 %all-to-all-start.1 = ((bf16[8,128,256]{2,1,0:T(8,128)(2,1)}), bf16[8,128,256]{2,1,0:T(8,128)(2,1)S(1)}, u32[]{:S(2)}, u32[]{:S(2)}) async-start(bf16[8,128,256]{2,1,0:T(8,128)(2,1)} %broadcast_in_dim.7), calls=%async_computation.1 | async-start | bytes 1048576 | tf_op jit(solution)/shard_map/all_to_all | solution.py:147
  65.4 3.2 %collective-permute-start.3 = (bf16[256,256]{1,0:T(8,128)(2,1)S(1)}, bf16[256,256]{1,0:T(8,128)(2,1)S(1)}, u32[]{:S(2)}, u32[]{:S(2)}) collective-permute-start(bf16[256,256]{1,0:T(8,128)(2,1)S(1)} %get-tuple-element.32), channel_id=1, source_target_pairs={{0,2},{2,4},{4,6},{6,0},{1,3},{3,5},{5,7},{7,1},{8,10},{10,12},{12... | collective-permute-start | bytes 393224 | tf_op jit(solution)/shard_map/ppermute | solution.py:183
  68.6 4.8 %collective-permute-start.4 = (bf16[256,256]{1,0:T(8,128)(2,1)S(1)}, bf16[256,256]{1,0:T(8,128)(2,1)S(1)}, u32[]{:S(2)}, u32[]{:S(2)}) collective-permute-start(bf16[256,256]{1,0:T(8,128)(2,1)S(1)} %get-tuple-element.31), channel_id=1, source_target_pairs={{0,6},{2,0},{4,2},{6,4},{1,7},{3,1},{5,3},{7,5},{8,14},{10,8},{12,... | collective-permute-start | bytes 393224 | tf_op jit(solution)/shard_map/ppermute | solution.py:183
  73.4 5.1 %collective-permute-start.5 = (bf16[256,256]{1,0:T(8,128)(2,1)S(1)}, bf16[256,256]{1,0:T(8,128)(2,1)S(1)}, u32[]{:S(2)}, u32[]{:S(2)}) collective-permute-start(bf16[256,256]{1,0:T(8,128)(2,1)S(1)} %get-tuple-element.30), channel_id=1, source_target_pairs={{0,4},{2,6},{4,0},{6,2},{1,5},{3,7},{5,1},{7,3},{8,12},{10,14},{12... | collective-permute-start | bytes 393224 | tf_op jit(solution)/shard_map/ppermute | solution.py:183
  78.5 5.7 %collective-permute-done.5 = bf16[256,256]{1,0:T(8,128)(2,1)S(1)} collective-permute-done((bf16[256,256]{1,0:T(8,128)(2,1)S(1)}, bf16[256,256]{1,0:T(8,128)(2,1)S(1)}, u32[]{:S(2)}, u32[]{:S(2)}) %collective-permute-start.5) | collective-permute-done | bytes 131104 | tf_op jit(solution)/shard_map/ppermute | solution.py:183
  84.3 0.8 broadcast_in_dim.8
  85.1 6.5 %all-to-all-start.2 = ((bf16[8,128,256]{2,1,0:T(8,128)(2,1)}), bf16[8,128,256]{2,1,0:T(8,128)(2,1)S(1)}, u32[]{:S(2)}, u32[]{:S(2)}) async-start(bf16[8,128,256]{2,1,0:T(8,128)(2,1)} %broadcast_in_dim.8), calls=%async_computation.2 | async-start | bytes 1048576 | tf_op jit(solution)/shard_map/all_to_all | solution.py:147
  91.7 5.5 %collective-permute-start.6 = (bf16[128,256]{1,0:T(8,128)(2,1)S(1)}, bf16[128,256]{1,0:T(8,128)(2,1)S(1)}, u32[]{:S(2)}, u32[]{:S(2)}) collective-permute-start(bf16[128,256]{1,0:T(8,128)(2,1)S(1)} %slice.13), channel_id=1, source_target_pairs={{0,256},{256,0},{1,257},{257,1},{2,258},{258,2},{3,259},{259,3},{4... | collective-permute-start | bytes 196616 | tf_op jit(solution)/shard_map/ppermute | solution.py:142
  97.2 5.1 %collective-permute-done.6 = bf16[128,256]{1,0:T(8,128)(2,1)S(1)} collective-permute-done((bf16[128,256]{1,0:T(8,128)(2,1)S(1)}, bf16[128,256]{1,0:T(8,128)(2,1)S(1)}, u32[]{:S(2)}, u32[]{:S(2)}) %collective-permute-start.6) | collective-permute-done | bytes 65568 | tf_op jit(solution)/shard_map/ppermute | solution.py:142
  102.3 0.7 slice_add_fusion
  103.0 1.1 %bitcast_convert_fusion = f32[1024,256]{1,0:T(8,128)} fusion(bf16[8,128,256]{2,1,0:T(8,128)(2,1)S(1)} %all-to-all-done.2), kind=kLoop, calls=%fused_computation.1 | loop fusion | flops 262144 | bytes 1572864 | tf_op jit(solution)/shard_map/convert_element_type | solution.py:192
  (23 shorter events, 0.8 us)
Async XLA Ops:
  0.6 6.7 %copy-start.4 = (s32[1,1,1,2048]{3,2,1,0:T(1,128)S(1)}, s32[1,1,1,2048]{3,2,1,0:T(1,128)}, u32[]{:S(2)}) copy-start(s32[1,1,1,2048]{3,2,1,0:T(1,128)} %param.12) | copy-start | bytes 24580
  0.6 11.3 %collective-permute-start = (bf16[128,256]{1,0:T(8,128)(2,1)}, bf16[128,256]{1,0:T(8,128)(2,1)S(1)}, u32[]{:S(2)}, u32[]{:S(2)}) collective-permute-start(bf16[128,256]{1,0:T(8,128)(2,1)} %param.7), channel_id=1, source_target_pairs={{0,256},{256,0},{1,257},{257,1},{2,258},{258,2},{3,259},{259,3},{4... | collective-permute-start | bytes 196616 | tf_op jit(solution)/shard_map/ppermute | solution.py:142
  7.3 0.7 copy-start.2
  8.0 1.2 %copy-start.3 = (f32[1024,256]{1,0:T(8,128)S(1)}, f32[1024,256]{1,0:T(8,128)}, u32[]{:S(2)}) copy-start(f32[1024,256]{1,0:T(8,128)} %table_ref.1) | copy-start | bytes 3145732
  9.2 2.7 %copy-start.5 = (bf16[128,256]{1,0:T(8,128)(2,1)S(1)}, bf16[128,256]{1,0:T(8,128)(2,1)}, u32[]{:S(2)}) copy-start(bf16[128,256]{1,0:T(8,128)(2,1)} %param.7) | copy-start | bytes 196612
  33.7 3.9 %copy-start.1 = (s32[1,1,512]{2,1,0:T(1,128)S(1)}, s32[1,1,512]{2,1,0:T(1,128)}, u32[]{:S(2)}) copy-start(s32[1,1,512]{2,1,0:T(1,128)} %param.10) | copy-start | bytes 6148
  33.7 3.9 %copy-start = (s32[1,1,512]{2,1,0:T(1,128)S(1)}, s32[1,1,512]{2,1,0:T(1,128)}, u32[]{:S(2)}) copy-start(s32[1,1,512]{2,1,0:T(1,128)} %param.9) | copy-start | bytes 6148
  33.7 3.9 %collective-permute-start.1 = (bf16[4,256,256]{2,1,0:T(8,128)(2,1)S(1)}, bf16[4,256,256]{2,1,0:T(8,128)(2,1)S(1)}, u32[]{:S(2)}, u32[]{:S(2)}) collective-permute-start(bf16[4,256,256]{2,1,0:T(8,128)(2,1)S(1)} %bitcast.18), channel_id=1, source_target_pairs={{0,1},{1,0},{2,3},{3,2},{4,5},{5,4},{6,7},{7,6},{8,9},{9,8},{10,11... | collective-permute-start | bytes 1572872 | tf_op jit(solution)/shard_map/ppermute | solution.py:142
  41.9 14.2 %all-to-all-start = ((bf16[8,128,256]{2,1,0:T(8,128)(2,1)}), bf16[8,128,256]{2,1,0:T(8,128)(2,1)S(1)}, u32[]{:S(2)}, u32[]{:S(2)}) async-start(bf16[8,128,256]{2,1,0:T(8,128)(2,1)} %get-tuple-element.23), calls=%async_computation | async-start | bytes 1048576 | tf_op jit(solution)/shard_map/all_to_all | solution.py:155
  47.7 3.8 %collective-permute-start.2 = (bf16[4,256,256]{2,1,0:T(8,128)(2,1)S(1)}, bf16[4,256,256]{2,1,0:T(8,128)(2,1)S(1)}, u32[]{:S(2)}, u32[]{:S(2)}) collective-permute-start(bf16[4,256,256]{2,1,0:T(8,128)(2,1)S(1)} %get-tuple-element.22), channel_id=1, source_target_pairs={{0,1},{1,0},{2,3},{3,2},{4,5},{5,4},{6,7},{7,6},{8,9},{9,8},{10,11... | collective-permute-start | bytes 1572872 | tf_op jit(solution)/shard_map/ppermute | solution.py:142
  56.9 27.3 %all-to-all-start.1 = ((bf16[8,128,256]{2,1,0:T(8,128)(2,1)}), bf16[8,128,256]{2,1,0:T(8,128)(2,1)S(1)}, u32[]{:S(2)}, u32[]{:S(2)}) async-start(bf16[8,128,256]{2,1,0:T(8,128)(2,1)} %broadcast_in_dim.7), calls=%async_computation.1 | async-start | bytes 1048576 | tf_op jit(solution)/shard_map/all_to_all | solution.py:147
  65.4 13.1 %collective-permute-start.3 = (bf16[256,256]{1,0:T(8,128)(2,1)S(1)}, bf16[256,256]{1,0:T(8,128)(2,1)S(1)}, u32[]{:S(2)}, u32[]{:S(2)}) collective-permute-start(bf16[256,256]{1,0:T(8,128)(2,1)S(1)} %get-tuple-element.32), channel_id=1, source_target_pairs={{0,2},{2,4},{4,6},{6,0},{1,3},{3,5},{5,7},{7,1},{8,10},{10,12},{12... | collective-permute-start | bytes 393224 | tf_op jit(solution)/shard_map/ppermute | solution.py:183
  68.6 9.9 %collective-permute-start.4 = (bf16[256,256]{1,0:T(8,128)(2,1)S(1)}, bf16[256,256]{1,0:T(8,128)(2,1)S(1)}, u32[]{:S(2)}, u32[]{:S(2)}) collective-permute-start(bf16[256,256]{1,0:T(8,128)(2,1)S(1)} %get-tuple-element.31), channel_id=1, source_target_pairs={{0,6},{2,0},{4,2},{6,4},{1,7},{3,1},{5,3},{7,5},{8,14},{10,8},{12,... | collective-permute-start | bytes 393224 | tf_op jit(solution)/shard_map/ppermute | solution.py:183
  73.4 10.8 %collective-permute-start.5 = (bf16[256,256]{1,0:T(8,128)(2,1)S(1)}, bf16[256,256]{1,0:T(8,128)(2,1)S(1)}, u32[]{:S(2)}, u32[]{:S(2)}) collective-permute-start(bf16[256,256]{1,0:T(8,128)(2,1)S(1)} %get-tuple-element.30), channel_id=1, source_target_pairs={{0,4},{2,6},{4,0},{6,2},{1,5},{3,7},{5,1},{7,3},{8,12},{10,14},{12... | collective-permute-start | bytes 393224 | tf_op jit(solution)/shard_map/ppermute | solution.py:183
  85.1 17.9 %all-to-all-start.2 = ((bf16[8,128,256]{2,1,0:T(8,128)(2,1)}), bf16[8,128,256]{2,1,0:T(8,128)(2,1)S(1)}, u32[]{:S(2)}, u32[]{:S(2)}) async-start(bf16[8,128,256]{2,1,0:T(8,128)(2,1)} %broadcast_in_dim.8), calls=%async_computation.2 | async-start | bytes 1048576 | tf_op jit(solution)/shard_map/all_to_all | solution.py:147
  91.7 10.6 %collective-permute-start.6 = (bf16[128,256]{1,0:T(8,128)(2,1)S(1)}, bf16[128,256]{1,0:T(8,128)(2,1)S(1)}, u32[]{:S(2)}, u32[]{:S(2)}) collective-permute-start(bf16[128,256]{1,0:T(8,128)(2,1)S(1)} %slice.13), channel_id=1, source_target_pairs={{0,256},{256,0},{1,257},{257,1},{2,258},{258,2},{3,259},{259,3},{4... | collective-permute-start | bytes 196616 | tf_op jit(solution)/shard_map/ppermute | solution.py:142

commit v3 on v2

v3 whole, which is shorter than its diff:
```python
import jax
import jax.numpy as jnp
from jax import lax
from jax.experimental import pallas as pl
from jax.experimental.pallas import tpu as pltpu
from jax.sharding import Mesh
from jax.sharding import PartitionSpec as P

F32 = jnp.float32
BF16 = jnp.bfloat16
AXES = ("yh", "yl", "x", "zl", "zh", "core")
NEAR = ("x", "zl")
FAR = ("yh", "yl")

D = 256
HALF = 128
SHARD = 128
EDGES = 512
CHUNK = 256
PARTS = 1024


def dot(a, b, ca, cb):
    return lax.dot_general(a, b, (((ca,), (cb,)), ((), ())), preferred_element_type=F32)


LHS, RHS, REL, NEG, LIVE = 0, 2, 4, 6, 14
PACK_ROWS = 16
NEGATIVES = 2048


def pack_ids(lhs, rhs, rel, neg, live):
    rest = jnp.zeros((PACK_ROWS * 256 - 3 * EDGES - NEGATIVES - 1,), jnp.int32)
    ids = jnp.concatenate([lhs, rhs, rel, neg, live, rest]).reshape(PACK_ROWS, 256)
    return jnp.concatenate([jnp.right_shift(ids, 5), jnp.bitwise_and(ids, 31)], axis=0).astype(BF16)


def unpack(block, start, stop):
    wide = block[SHARD:].astype(F32)
    ids = wide[:PACK_ROWS] * 32.0 + wide[PACK_ROWS:]
    return jnp.concatenate([ids[k:k + 1] for k in range(start, stop)], axis=1).astype(jnp.int32)


def place(ids, core):
    owner = jnp.bitwise_and(jnp.right_shift(ids, 7), 1)
    side = jnp.where(owner == core, 0, 512)
    return side + jnp.right_shift(ids, 8) * SHARD + jnp.bitwise_and(ids, SHARD - 1)


def one_hot(ids, step):
    rows = lax.broadcasted_iota(jnp.int32, (CHUNK, EDGES), 0)
    return (rows == ids - step * CHUNK).astype(F32).astype(BF16)


def early_kernel(core_ref, block_ref, table_ref, w_out, counts_out):
    lane_rows = lax.broadcasted_iota(jnp.int32, (CHUNK, 128), 0)
    block = block_ref[...]
    rel = unpack(block, REL, NEG)
    neg = place(unpack(block, NEG, LIVE), core_ref[0])
    w = jnp.zeros((D, EDGES), F32)
    for step in range(PARTS // CHUNK):
        table = table_ref[step * CHUNK:(step + 1) * CHUNK, :]
        high = table.astype(BF16)
        low = (table - high.astype(F32)).astype(BF16)
        hot = one_hot(rel, step)
        w = w + dot(high, hot, 0, 0) + dot(low, hot, 0, 0)
        found = jnp.zeros((CHUNK, 128), F32)
        for k in range(NEGATIVES // 128):
            found = found + (lane_rows == neg[:, k * 128:(k + 1) * 128] - step * CHUNK).astype(F32)
        counts_out[step * CHUNK:(step + 1) * CHUNK, :] = jnp.broadcast_to(
            jnp.sum(found, axis=1, keepdims=True) * NEGATIVES ** (-0.5), (CHUNK, 128)
        )
    w_out[...] = w


def edge_kernel(
    core_ref, zh_ref, block_a, block_b, w_a, w_b, counts_a, counts_b, mine_ref, other_ref,
    mine_out, other_out, rel_out,
):
    core, zh = core_ref[0], zh_ref[0]
    pack_a, pack_b = block_a[...], block_b[...]
    rows = lax.broadcasted_iota(jnp.int32, (CHUNK, EDGES), 0)
    lanes = lax.broadcasted_iota(jnp.int32, (1, EDGES), 1)
    steps = range(PARTS // CHUNK)

    def chunk_of(part, step):
        ref = mine_ref if step < 2 else other_ref
        s = 2 * (step % 2)
        here = slice(part * SHARD, (part + 1) * SHARD)
        return jnp.concatenate([ref[s, here], ref[s + 1, here]], axis=0)

    def queries(pack, w_ref, head_part):
        lhs = place(unpack(pack, LHS, RHS), core)
        rhs = place(unpack(pack, RHS, REL), core)
        alive = (lanes < unpack(pack, LIVE, LIVE + 1)[:, :1]).astype(F32)
        h = jnp.zeros((D, EDGES), F32)
        t = jnp.zeros((D, EDGES), F32)
        for step in steps:
            h = h + dot(chunk_of(head_part, step), one_hot(lhs, step), 0, 0)
            t = t + dot(chunk_of(1 - head_part, step), one_hot(rhs, step), 0, 0)
        w_re, w_im, h_re, h_im = w_ref[:HALF], w_ref[HALF:], h[:HALF], h[HALF:]
        query = jnp.concatenate(
            [h_re * w_re - h_im * w_im, h_re * w_im + h_im * w_re], axis=0
        ).astype(BF16)
        pos = jnp.sum(query.astype(F32) * t, axis=0, keepdims=True)
        pos_grad = (0.5 * jnp.tanh(0.5 * pos) - 0.5) * alive
        return lhs, rhs, alive, h, query, pos_grad

    def score_grads(tails, query, counts_ref, step, rhs, alive, pos_grad):
        scores = dot(tails, query, 1, 0)
        often = counts_ref[step * CHUNK:(step + 1) * CHUNK, :]
        often = jnp.concatenate([often] * (EDGES // 128), axis=1)
        both = (0.5 * jnp.tanh(0.5 * scores) + 0.5) * often * alive
        return (both + jnp.where(rows == rhs - step * CHUNK, pos_grad, 0.0)).astype(BF16)

    lhs, rhs, alive, h, query, pos_grad = queries(pack_a, w_a, 0)
    grad = jnp.zeros((D, EDGES), F32)
    for step in steps:
        tails = chunk_of(1, step)
        both = score_grads(tails, query, counts_a, step, rhs, alive, pos_grad)
        grad = grad + dot(tails, both, 0, 0)
    g_re, g_im = grad[:HALF], grad[HALF:]
    h_re, h_im, w_re, w_im = h[:HALF], h[HALF:], w_a[:HALF], w_a[HALF:]
    term = jnp.concatenate([g_re * h_re + g_im * h_im, g_im * h_re - g_re * h_im], axis=0).astype(BF16)
    head = jnp.concatenate([g_re * w_re + g_im * w_im, g_im * w_re - g_re * w_im], axis=0).astype(BF16)

    _, rhs, alive, _, query, pos_grad = queries(pack_b, w_b, 1)
    rel = unpack(pack_a, REL, NEG)
    for step in steps:
        both = score_grads(chunk_of(0, step), query, counts_b, step, rhs, alive, pos_grad)
        out = (dot(both, query, 1, 1) + dot(one_hot(lhs, step), head, 1, 1)).astype(BF16)
        for half in range(2):
            d = jnp.bitwise_and(2 * (step % 2) + half - zh, 3)
            ref = mine_out if step < 2 else other_out
            ref[d] = out[half * SHARD:(half + 1) * SHARD]
        out = dot(one_hot(rel, step), term, 1, 1).astype(BF16)
        rel_out[2 * step] = out[:SHARD]
        rel_out[2 * step + 1] = out[SHARD:]


def early_terms(core, block, table):
    vmem = pl.BlockSpec(memory_space=pltpu.VMEM)
    return pl.pallas_call(
        early_kernel,
        out_shape=(jax.ShapeDtypeStruct((D, EDGES), F32), jax.ShapeDtypeStruct((PARTS, 128), F32)),
        in_specs=[pl.BlockSpec(memory_space=pltpu.SMEM)] + [vmem] * 2,
        out_specs=(vmem, vmem),
        compiler_params=pltpu.CompilerParams(vmem_limit_bytes=24 << 20),
        cost_estimate=pl.CostEstimate(flops=1 << 30, bytes_accessed=3 << 20, transcendentals=0),
    )(core, block, table)


def edge_terms(core, zh, block_a, block_b, w_a, w_b, counts_a, counts_b, mine, other):
    vmem = pl.BlockSpec(memory_space=pltpu.VMEM)
    block = jax.ShapeDtypeStruct((4, SHARD, D), BF16)
    return pl.pallas_call(
        edge_kernel,
        out_shape=(block, block, jax.ShapeDtypeStruct((8, SHARD, D), BF16)),
        in_specs=[pl.BlockSpec(memory_space=pltpu.SMEM)] * 2 + [vmem] * 8,
        out_specs=(vmem, vmem, vmem),
        compiler_params=pltpu.CompilerParams(vmem_limit_bytes=40 << 20),
    )(core, zh, block_a, block_b, w_a, w_b, counts_a, counts_b, mine, other)


def swap(block, axis, distance=1):
    size = lax.axis_size(axis)
    return lax.ppermute(block, axis, [(i, i ^ distance) for i in range(size)])


def spread(block, axis, size):
    copies = jnp.broadcast_to(block[None], (size,) + block.shape)
    return lax.all_to_all(copies, axis, 0, 0)


def summed(blocks):
    return jnp.sum(blocks.astype(F32), axis=0).astype(BF16)


def exchange(blocks, axis):
    return lax.all_to_all(blocks, axis, 0, 0)


def tie(*values):
    return lax.optimization_barrier(values)


def local(embeddings, relations, lhs_ids, rhs_ids, rel_ids, neg_ids, live):
    core = lax.axis_index("core").astype(jnp.int32)[None]
    zh = lax.axis_index("zh").astype(jnp.int32)[None]
    ids = pack_ids(lhs_ids[0, 0], rhs_ids[0, 0], rel_ids[0, 0], neg_ids[0, 0, 0], live)
    block_a = jnp.concatenate([embeddings, ids], axis=0)
    block_b = swap(block_a, "yh")
    w_a, counts_a = early_terms(core, block_a, relations)
    block_b, w_a, counts_a = tie(block_b, w_a, counts_a)
    both = jnp.concatenate([embeddings, block_b[:SHARD]], axis=0)
    mine = lax.all_gather(both, "zh", axis=0, tiled=False)
    other = swap(mine, "core")
    w_b, counts_b = early_terms(core, block_b, relations)
    mine_sum, other_sum, rel_part = edge_terms(
        core, zh, block_a, block_b, w_a, w_b, counts_a, counts_b, mine, other
    )
    from_core = swap(other_sum, "core")
    parts = exchange(rel_part, NEAR)
    from_core, parts = tie(from_core, parts)
    chip = (mine_sum.astype(F32) + from_core.astype(F32)).astype(BF16)
    arrived = [
        lax.ppermute(chip[step], "zh", [(i, (i + step) % 4) for i in range(4)]) for step in (1, 3, 2)
    ]
    parts = spread(summed(parts), FAR, 8)
    *arrived, parts = tie(*arrived, parts)
    shard = chip[0].astype(F32)
    for block in arrived:
        shard = shard + block.astype(F32)
    rel_all = spread(summed(parts), NEAR, 8).reshape(PARTS, D)
    return shard, rel_all.astype(F32)


def solution(mesh):
    fine = Mesh(mesh.devices.reshape(2, 4, 4, 2, 4, 2), AXES)
    dom, rel = AXES[:4], AXES[4:]
    placed = (
        P(AXES, None),
        P(rel, None),
        P(dom, rel, None),
        P(dom, rel, None),
        P(dom, rel, None),
        P(dom, rel, None, None),
        P(AXES),
    )
    return jax.shard_map(
        local,
        mesh=fine,
        in_specs=placed,
        out_specs=(P(AXES, None), P(rel, None)),
        check_vma=False,
    )
```

time: 105 us -> 102 us (0.971)
  the two profiles are of different devices: /device:TPU:18 before, /device:TPU:1 now
where the time goes in v3:
time: 102 us
  starting transfers between devices  45.9 us (45%)
  waiting for transfers between devices  20.7 us (20%)
  blocking collectives  19.1 us (19%)
  Pallas kernels  8.91 us (9%)
  local copies, waits for them, and re-layouts  3.74 us (4%)
  other arithmetic  2 us (2%)
  between operations  1.5 us (1%)
    all_gather x1, blocking collectives, local(): mine = lax.all_gather(both, 'zh', axis=0, tiled=False)  19.1 us
    ppermute x3, starting transfers between devices, swap(): return lax.ppermute(block, axis, [(i, i ^ distance) for i in range(size)])  15.8 us
    all_to_all x2, starting transfers between devices, spread(): return lax.all_to_all(copies, axis, 0, 0)  12.8 us
    ppermute x3, starting transfers between devices, local(): lax.ppermute(chip[step], 'zh', [(i, (i + step) % 4) for i in range(4)])  11.1 us
    all_to_all x2, waiting for transfers between devices, spread(): return lax.all_to_all(copies, axis, 0, 0)  8.96 us
    all_to_all x1, waiting for transfers between devices, exchange(): return lax.all_to_all(blocks, axis, 0, 0)  6.21 us
    all_to_all x1, starting transfers between devices, exchange(): return lax.all_to_all(blocks, axis, 0, 0)  6.21 us
    pallas_call x1, Pallas kernels, edge_terms(): pl.pallas_call(edge_kernel, out_shape=(block, block, jax.ShapeDtypeStruct...  5.04 us
  transfers between devices with their start and end apart: 9, of which 6 were waited for; matrix products, arithmetic and copies ran while one was open for 1% of the time, Pallas kernels for 4%

profile of v3, /device:TPU:1, one launch (start us, length us, event | category | flops | bytes accessed | tf_op | source)
XLA Modules:
  0.0 101.9 jit_solution(785417343711777242)
XLA Ops:
  1.3 0.8 concatenate.12
  2.2 8.3 %collective-permute-start = (bf16[160,256]{1,0:T(8,128)(2,1)S(1)}, bf16[160,256]{1,0:T(8,128)(2,1)S(1)}, u32[]{:S(2)}, u32[]{:S(2)}) collective-permute-start(bf16[160,256]{1,0:T(8,128)(2,1)S(1)} %constant_dynamic-update-slice_fusion.block_ref.block_a), channel_id=1, source_target_pairs={{0,256},{256,0},{1,257},{257,1},{2,258},{258,2},{3,259},{259,3},{4... | collective-permute-start | bytes 245768 | tf_op jit(solution)/shard_map/ppermute | solution.py:167
  10.5 1.2 %copy-done = f32[1024,256]{1,0:T(8,128)S(1)} copy-done((f32[1024,256]{1,0:T(8,128)S(1)}, f32[1024,256]{1,0:T(8,128)}, u32[]{:S(2)}) %copy-start) | copy-done | bytes 1048600
  11.7 1.9 %shard_map.86 = (f32[256,512]{1,0:T(8,128)S(1)}, f32[1024,128]{1,0:T(8,128)S(1)}) custom-call(s32[1]{0:T(128)} %bitcast.core_ref, bf16[160,256]{1,0:T(8,128)(2,1)S(1)} %constant_dynamic-update-slice_fusion.block_ref.block_a, f32[1024,256]{1,0:T(8,128)S(1)} %copy-done), custom_call_target="tpu_custom_call" | custom-call | flops 1073741824 | bytes 3145728 | tf_op jit(solution)/shard_map/pallas_call | solution.py:143
  13.7 19.1 %all-gather = bf16[1024,256]{1,0:T(8,128)(2,1)S(1)} all-gather(bf16[256,256]{1,0:T(8,128)(2,1)S(1)} %pad_maximum_fusion), channel_id=2, replica_groups=mesh['yh'=2,'yl'=4,'x'=4,'zl'=2,'zh'=4,'core'=2] {'zh'}, dimensions={0}, use_global_device_ids=true | all-gather | bytes 655360 | tf_op jit(solution)/shard_map/all_gather | solution.py:196
  32.9 5.3 %collective-permute-start.1 = (bf16[4,256,256]{2,1,0:T(8,128)(2,1)S(1)}, bf16[4,256,256]{2,1,0:T(8,128)(2,1)S(1)}, u32[]{:S(2)}, u32[]{:S(2)}) collective-permute-start(bf16[4,256,256]{2,1,0:T(8,128)(2,1)S(1)} %bitcast.21), channel_id=1, source_target_pairs={{0,1},{1,0},{2,3},{3,2},{4,5},{5,4},{6,7},{7,6},{8,9},{9,8},{10,11... | collective-permute-start | bytes 1572872 | tf_op jit(solution)/shard_map/ppermute | solution.py:167
  38.2 1.9 %shard_map.87 = (f32[256,512]{1,0:T(8,128)S(1)}, f32[1024,128]{1,0:T(8,128)S(1)}) custom-call(s32[1]{0:T(128)} %bitcast.core_ref, bf16[160,256]{1,0:T(8,128)(2,1)S(1)} %collective-permute-done.block_ref.block_b, f32[1024,256]{1,0:T(8,128)S(1)} %copy-done.1), custom_call_target="tpu_custom_call" | custom-call | flops 1073741824 | bytes 3145728 | tf_op jit(solution)/shard_map/pallas_call | solution.py:143
  40.2 5.0 %shard_map.88 = (bf16[4,128,256]{2,1,0:T(8,128)(2,1)S(1)}, bf16[4,128,256]{2,1,0:T(8,128)(2,1)S(1)}, bf16[8,128,256]{2,1,0:T(8,128)(2,1)}) custom-call(s32[1]{0:T(128)} %bitcast.core_ref, s32[1]{0:T(128)} %bitcast.1.zh_ref, bf16[160,256]{1,0:T(8,128)(2,1)S(1)} %constant_dynamic-update-slice_fusion.block_ref.block_a, ...), custom_call_target="tpu_custom_call" | custom-call | tf_op jit(solution)/shard_map/pallas_call | solution.py:156
  45.2 6.2 %all-to-all-start = ((bf16[8,128,256]{2,1,0:T(8,128)(2,1)}), bf16[8,128,256]{2,1,0:T(8,128)(2,1)S(1)}, u32[]{:S(2)}, u32[]{:S(2)}) async-start(bf16[8,128,256]{2,1,0:T(8,128)(2,1)} %get-tuple-element.27), calls=%async_computation | async-start | bytes 1048576 | tf_op jit(solution)/shard_map/all_to_all | solution.py:180
  51.4 2.2 %collective-permute-start.2 = (bf16[4,128,256]{2,1,0:T(8,128)(2,1)S(1)}, bf16[4,128,256]{2,1,0:T(8,128)(2,1)S(1)}, u32[]{:S(2)}, u32[]{:S(2)}) collective-permute-start(bf16[4,128,256]{2,1,0:T(8,128)(2,1)S(1)} %get-tuple-element.26), channel_id=1, source_target_pairs={{0,1},{1,0},{2,3},{3,2},{4,5},{5,4},{6,7},{7,6},{8,9},{9,8},{10,11... | collective-permute-start | bytes 786440 | tf_op jit(solution)/shard_map/ppermute | solution.py:167
  53.6 1.2 %collective-permute-done.2 = bf16[4,128,256]{2,1,0:T(8,128)(2,1)S(1)} collective-permute-done((bf16[4,128,256]{2,1,0:T(8,128)(2,1)S(1)}, bf16[4,128,256]{2,1,0:T(8,128)(2,1)S(1)}, u32[]{:S(2)}, u32[]{:S(2)}) %collective-permute-start.2) | collective-permute-done | bytes 262176 | tf_op jit(solution)/shard_map/ppermute | solution.py:167
  54.8 6.2 %all-to-all-done = bf16[8,128,256]{2,1,0:T(8,128)(2,1)S(1)} async-done(((bf16[8,128,256]{2,1,0:T(8,128)(2,1)}), bf16[8,128,256]{2,1,0:T(8,128)(2,1)S(1)}, u32[]{:S(2)}, u32[]{:S(2)}) %all-to-all-start) | async-done | bytes 524320 | tf_op jit(solution)/shard_map/all_to_all | solution.py:180
  61.1 0.8 broadcast_in_dim.24
  62.0 7.4 %all-to-all-start.1 = ((bf16[8,128,256]{2,1,0:T(8,128)(2,1)}), bf16[8,128,256]{2,1,0:T(8,128)(2,1)S(1)}, u32[]{:S(2)}, u32[]{:S(2)}) async-start(bf16[8,128,256]{2,1,0:T(8,128)(2,1)} %broadcast_in_dim.24), calls=%async_computation.1 | async-start | bytes 1048576 | tf_op jit(solution)/shard_map/all_to_all | solution.py:172
  69.4 4.9 %collective-permute-start.5 = (bf16[128,256]{1,0:T(8,128)(2,1)S(1)}, bf16[128,256]{1,0:T(8,128)(2,1)S(1)}, u32[]{:S(2)}, u32[]{:S(2)}) collective-permute-start(bf16[128,256]{1,0:T(8,128)(2,1)S(1)} %get-tuple-element.34), channel_id=1, source_target_pairs={{0,4},{2,6},{4,0},{6,2},{1,5},{3,7},{5,1},{7,3},{8,12},{10,14},{12... | collective-permute-start | bytes 196616 | tf_op jit(solution)/shard_map/ppermute | solution.py:207
  74.3 3.3 %collective-permute-start.4 = (bf16[128,256]{1,0:T(8,128)(2,1)S(1)}, bf16[128,256]{1,0:T(8,128)(2,1)S(1)}, u32[]{:S(2)}, u32[]{:S(2)}) collective-permute-start(bf16[128,256]{1,0:T(8,128)(2,1)S(1)} %get-tuple-element.35), channel_id=1, source_target_pairs={{0,6},{2,0},{4,2},{6,4},{1,7},{3,1},{5,3},{7,5},{8,14},{10,8},{12,... | collective-permute-start | bytes 196616 | tf_op jit(solution)/shard_map/ppermute | solution.py:207
  77.6 2.9 %collective-permute-start.3 = (bf16[128,256]{1,0:T(8,128)(2,1)S(1)}, bf16[128,256]{1,0:T(8,128)(2,1)S(1)}, u32[]{:S(2)}, u32[]{:S(2)}) collective-permute-start(bf16[128,256]{1,0:T(8,128)(2,1)S(1)} %get-tuple-element.36), channel_id=1, source_target_pairs={{0,2},{2,4},{4,6},{6,0},{1,3},{3,5},{5,7},{7,1},{8,10},{10,12},{12... | collective-permute-start | bytes 196616 | tf_op jit(solution)/shard_map/ppermute | solution.py:207
  80.5 1.2 %collective-permute-done.4 = bf16[128,256]{1,0:T(8,128)(2,1)S(1)} collective-permute-done((bf16[128,256]{1,0:T(8,128)(2,1)S(1)}, bf16[128,256]{1,0:T(8,128)(2,1)S(1)}, u32[]{:S(2)}, u32[]{:S(2)}) %collective-permute-start.4) | collective-permute-done | bytes 65568 | tf_op jit(solution)/shard_map/ppermute | solution.py:207
  81.8 3.0 %collective-permute-done.3 = bf16[128,256]{1,0:T(8,128)(2,1)S(1)} collective-permute-done((bf16[128,256]{1,0:T(8,128)(2,1)S(1)}, bf16[128,256]{1,0:T(8,128)(2,1)S(1)}, u32[]{:S(2)}, u32[]{:S(2)}) %collective-permute-start.3) | collective-permute-done | bytes 65568 | tf_op jit(solution)/shard_map/ppermute | solution.py:207
  85.4 0.8 broadcast_in_dim.25
  86.2 5.4 %all-to-all-start.2 = ((bf16[8,128,256]{2,1,0:T(8,128)(2,1)}), bf16[8,128,256]{2,1,0:T(8,128)(2,1)S(1)}, u32[]{:S(2)}, u32[]{:S(2)}) async-start(bf16[8,128,256]{2,1,0:T(8,128)(2,1)} %broadcast_in_dim.25), calls=%async_computation.2 | async-start | bytes 1048576 | tf_op jit(solution)/shard_map/all_to_all | solution.py:172
  91.6 0.7 fusion.1
  92.3 8.5 %all-to-all-done.2 = bf16[8,128,256]{2,1,0:T(8,128)(2,1)S(1)} async-done(((bf16[8,128,256]{2,1,0:T(8,128)(2,1)}), bf16[8,128,256]{2,1,0:T(8,128)(2,1)S(1)}, u32[]{:S(2)}, u32[]{:S(2)}) %all-to-all-start.2) | async-done | bytes 524320 | tf_op jit(solution)/shard_map/all_to_all | solution.py:172
  100.8 1.1 %bitcast_convert_fusion = f32[1024,256]{1,0:T(8,128)} fusion(bf16[8,128,256]{2,1,0:T(8,128)(2,1)S(1)} %all-to-all-done.2), kind=kLoop, calls=%fused_computation | loop fusion | flops 262144 | bytes 1572864 | tf_op jit(solution)/shard_map/convert_element_type | solution.py:215
  (24 shorter events, 0.8 us)
Async XLA Ops:
  0.6 0.7 copy-start.3
  0.6 1.5 %copy-start.2 = (bf16[128,256]{1,0:T(8,128)(2,1)S(1)}, bf16[128,256]{1,0:T(8,128)(2,1)}, u32[]{:S(2)}) copy-start(bf16[128,256]{1,0:T(8,128)(2,1)} %param.7) | copy-start | bytes 196612
  2.2 11.5 %collective-permute-start = (bf16[160,256]{1,0:T(8,128)(2,1)S(1)}, bf16[160,256]{1,0:T(8,128)(2,1)S(1)}, u32[]{:S(2)}, u32[]{:S(2)}) collective-permute-start(bf16[160,256]{1,0:T(8,128)(2,1)S(1)} %constant_dynamic-update-slice_fusion.block_ref.block_a), channel_id=1, source_target_pairs={{0,256},{256,0},{1,257},{257,1},{2,258},{258,2},{3,259},{259,3},{4... | collective-permute-start | bytes 245768 | tf_op jit(solution)/shard_map/ppermute | solution.py:167
  10.5 1.2 %copy-start = (f32[1024,256]{1,0:T(8,128)S(1)}, f32[1024,256]{1,0:T(8,128)}, u32[]{:S(2)}) copy-start(f32[1024,256]{1,0:T(8,128)} %table_ref.3) | copy-start | bytes 3145732
  13.7 24.5 %copy-start.1 = (f32[1024,256]{1,0:T(8,128)S(1)}, f32[1024,256]{1,0:T(8,128)}, u32[]{:S(2)}) copy-start(f32[1024,256]{1,0:T(8,128)} %table_ref.3) | copy-start | bytes 3145732
  32.9 7.3 %collective-permute-start.1 = (bf16[4,256,256]{2,1,0:T(8,128)(2,1)S(1)}, bf16[4,256,256]{2,1,0:T(8,128)(2,1)S(1)}, u32[]{:S(2)}, u32[]{:S(2)}) collective-permute-start(bf16[4,256,256]{2,1,0:T(8,128)(2,1)S(1)} %bitcast.21), channel_id=1, source_target_pairs={{0,1},{1,0},{2,3},{3,2},{4,5},{5,4},{6,7},{7,6},{8,9},{9,8},{10,11... | collective-permute-start | bytes 1572872 | tf_op jit(solution)/shard_map/ppermute | solution.py:167
  45.2 15.8 %all-to-all-start = ((bf16[8,128,256]{2,1,0:T(8,128)(2,1)}), bf16[8,128,256]{2,1,0:T(8,128)(2,1)S(1)}, u32[]{:S(2)}, u32[]{:S(2)}) async-start(bf16[8,128,256]{2,1,0:T(8,128)(2,1)} %get-tuple-element.27), calls=%async_computation | async-start | bytes 1048576 | tf_op jit(solution)/shard_map/all_to_all | solution.py:180
  51.4 3.4 %collective-permute-start.2 = (bf16[4,128,256]{2,1,0:T(8,128)(2,1)S(1)}, bf16[4,128,256]{2,1,0:T(8,128)(2,1)S(1)}, u32[]{:S(2)}, u32[]{:S(2)}) collective-permute-start(bf16[4,128,256]{2,1,0:T(8,128)(2,1)S(1)} %get-tuple-element.26), channel_id=1, source_target_pairs={{0,1},{1,0},{2,3},{3,2},{4,5},{5,4},{6,7},{7,6},{8,9},{9,8},{10,11... | collective-permute-start | bytes 786440 | tf_op jit(solution)/shard_map/ppermute | solution.py:167
  62.0 23.3 %all-to-all-start.1 = ((bf16[8,128,256]{2,1,0:T(8,128)(2,1)}), bf16[8,128,256]{2,1,0:T(8,128)(2,1)S(1)}, u32[]{:S(2)}, u32[]{:S(2)}) async-start(bf16[8,128,256]{2,1,0:T(8,128)(2,1)} %broadcast_in_dim.24), calls=%async_computation.1 | async-start | bytes 1048576 | tf_op jit(solution)/shard_map/all_to_all | solution.py:172
  69.4 11.1 %collective-permute-start.5 = (bf16[128,256]{1,0:T(8,128)(2,1)S(1)}, bf16[128,256]{1,0:T(8,128)(2,1)S(1)}, u32[]{:S(2)}, u32[]{:S(2)}) collective-permute-start(bf16[128,256]{1,0:T(8,128)(2,1)S(1)} %get-tuple-element.34), channel_id=1, source_target_pairs={{0,4},{2,6},{4,0},{6,2},{1,5},{3,7},{5,1},{7,3},{8,12},{10,14},{12... | collective-permute-start | bytes 196616 | tf_op jit(solution)/shard_map/ppermute | solution.py:207
  74.3 7.4 %collective-permute-start.4 = (bf16[128,256]{1,0:T(8,128)(2,1)S(1)}, bf16[128,256]{1,0:T(8,128)(2,1)S(1)}, u32[]{:S(2)}, u32[]{:S(2)}) collective-permute-start(bf16[128,256]{1,0:T(8,128)(2,1)S(1)} %get-tuple-element.35), channel_id=1, source_target_pairs={{0,6},{2,0},{4,2},{6,4},{1,7},{3,1},{5,3},{7,5},{8,14},{10,8},{12,... | collective-permute-start | bytes 196616 | tf_op jit(solution)/shard_map/ppermute | solution.py:207
  77.6 7.2 %collective-permute-start.3 = (bf16[128,256]{1,0:T(8,128)(2,1)S(1)}, bf16[128,256]{1,0:T(8,128)(2,1)S(1)}, u32[]{:S(2)}, u32[]{:S(2)}) collective-permute-start(bf16[128,256]{1,0:T(8,128)(2,1)S(1)} %get-tuple-element.36), channel_id=1, source_target_pairs={{0,2},{2,4},{4,6},{6,0},{1,3},{3,5},{5,7},{7,1},{8,10},{10,12},{12... | collective-permute-start | bytes 196616 | tf_op jit(solution)/shard_map/ppermute | solution.py:207
  86.2 14.6 %all-to-all-start.2 = ((bf16[8,128,256]{2,1,0:T(8,128)(2,1)}), bf16[8,128,256]{2,1,0:T(8,128)(2,1)S(1)}, u32[]{:S(2)}, u32[]{:S(2)}) async-start(bf16[8,128,256]{2,1,0:T(8,128)(2,1)} %broadcast_in_dim.25), calls=%async_computation.2 | async-start | bytes 1048576 | tf_op jit(solution)/shard_map/all_to_all | solution.py:172

commit v4 on v3

--- a/solution.py
+++ b/solution.py
@@ -8,9 +8,9 @@
 
 F32 = jnp.float32
 BF16 = jnp.bfloat16
-AXES = ("yh", "yl", "x", "zl", "zh", "core")
-NEAR = ("x", "zl")
-FAR = ("yh", "yl")
+AXES = ("yh", "ym", "yl", "x", "zl", "zh", "core")
+NEAR = ("yl", "x", "zl")
+FAR = ("yh", "ym")
 
 D = 256
 HALF = 128
@@ -134,8 +134,8 @@
             ref = mine_out if step < 2 else other_out
             ref[d] = out[half * SHARD:(half + 1) * SHARD]
         out = dot(one_hot(rel, step), term, 1, 1).astype(BF16)
-        rel_out[2 * step] = out[:SHARD]
-        rel_out[2 * step + 1] = out[SHARD:]
+        for quarter in range(4):
+            rel_out[4 * step + quarter] = out[quarter * 64:(quarter + 1) * 64]
 
 
 def early_terms(core, block, table):
@@ -155,7 +155,7 @@
     block = jax.ShapeDtypeStruct((4, SHARD, D), BF16)
     return pl.pallas_call(
         edge_kernel,
-        out_shape=(block, block, jax.ShapeDtypeStruct((8, SHARD, D), BF16)),
+        out_shape=(block, block, jax.ShapeDtypeStruct((16, 64, D), BF16)),
         in_specs=[pl.BlockSpec(memory_space=pltpu.SMEM)] * 2 + [vmem] * 8,
         out_specs=(vmem, vmem, vmem),
         compiler_params=pltpu.CompilerParams(vmem_limit_bytes=40 << 20),
@@ -165,6 +165,10 @@
 def swap(block, axis, distance=1):
     size = lax.axis_size(axis)
     return lax.ppermute(block, axis, [(i, i ^ distance) for i in range(size)])
+
+
+def move(block, step):
+    return lax.ppermute(block, "zh", [(i, (i + step) % 4) for i in range(4)])
 
 
 def spread(block, axis, size):
@@ -201,23 +205,19 @@
     )
     from_core = swap(other_sum, "core")
     parts = exchange(rel_part, NEAR)
-    from_core, parts = tie(from_core, parts)
-    chip = (mine_sum.astype(F32) + from_core.astype(F32)).astype(BF16)
-    arrived = [
-        lax.ppermute(chip[step], "zh", [(i, (i + step) % 4) for i in range(4)]) for step in (1, 3, 2)
-    ]
-    parts = spread(summed(parts), FAR, 8)
-    *arrived, parts = tie(*arrived, parts)
-    shard = chip[0].astype(F32)
-    for block in arrived:
-        shard = shard + block.astype(F32)
-    rel_all = spread(summed(parts), NEAR, 8).reshape(PARTS, D)
+    chip = mine_sum.astype(F32) + from_core.astype(F32)
+    two = move(chip[2], 2)
+    one, three = move(chip[1].astype(BF16), 1), move(chip[3].astype(BF16), 3)
+    parts = spread(summed(parts), FAR, 4)
+    two, one, parts = tie(two, one, parts)
+    shard = chip[0] + two + one.astype(F32) + three.astype(F32)
+    rel_all = spread(summed(parts), NEAR, 16).reshape(PARTS, D)
     return shard, rel_all.astype(F32)
 
 
 def solution(mesh):
-    fine = Mesh(mesh.devices.reshape(2, 4, 4, 2, 4, 2), AXES)
-    dom, rel = AXES[:4], AXES[4:]
+    fine = Mesh(mesh.devices.reshape(2, 2, 2, 4, 2, 4, 2), AXES)
+    dom, rel = AXES[:5], AXES[5:]
     placed = (
         P(AXES, None),
         P(rel, None),

time: 102 us -> 96.9 us (0.950)
  the two profiles are of different devices: /device:TPU:1 before, /device:TPU:16 now
where the time goes in v4:
time: 96.9 us; the launch traced here: 96.2 us
  starting transfers between devices  40.7 us (42%)
  blocking collectives  22.6 us (23%)
  waiting for transfers between devices  16.9 us (17%)
  Pallas kernels  8.91 us (9%)
  local copies, waits for them, and re-layouts  3.6 us (4%)
  other arithmetic  1.94 us (2%)
  between operations  1.51 us (2%)
    all_gather x1, blocking collectives, local(): mine = lax.all_gather(both, 'zh', axis=0, tiled=False)  22.6 us
    all_to_all x2, starting transfers between devices, spread(): return lax.all_to_all(copies, axis, 0, 0)  13.1 us
    ppermute x3, starting transfers between devices, move(): return lax.ppermute(block, 'zh', [(i, (i + step) % 4) for i in range(4)])  12.2 us
    ppermute x3, starting transfers between devices, swap(): return lax.ppermute(block, axis, [(i, i ^ distance) for i in range(size)])  9.97 us
    ppermute x3, waiting for transfers between devices, move(): return lax.ppermute(block, 'zh', [(i, (i + step) % 4) for i in range(4)])  9.28 us
    all_to_all x1, starting transfers between devices, exchange(): return lax.all_to_all(blocks, axis, 0, 0)  5.44 us
    pallas_call x1, Pallas kernels, edge_terms(): pl.pallas_call(edge_kernel, out_shape=(block, block, jax.ShapeDtypeStruct...  5.04 us
    pallas_call x2, Pallas kernels, early_terms(): pl.pallas_call(early_kernel, out_shape=(jax.ShapeDtypeStruct((D, EDGES),...  3.87 us
  transfers between devices with their start and end apart: 9, of which 6 were waited for; matrix products, arithmetic and copies ran while one was open for 2% of the time, Pallas kernels for 4%

profile of v4, /device:TPU:16, one launch (start us, length us, event | category | flops | bytes accessed | tf_op | source)
XLA Modules:
  0.0 96.2 jit_solution(31787626434214167)
XLA Ops:
  1.3 0.8 concatenate.12
  2.2 5.9 %collective-permute-start = (bf16[160,256]{1,0:T(8,128)(2,1)S(1)}, bf16[160,256]{1,0:T(8,128)(2,1)S(1)}, u32[]{:S(2)}, u32[]{:S(2)}) collective-permute-start(bf16[160,256]{1,0:T(8,128)(2,1)S(1)} %constant_dynamic-update-slice_fusion.block_ref.block_a), channel_id=1, source_target_pairs={{0,256},{256,0},{1,257},{257,1},{2,258},{258,2},{3,259},{259,3},{4... | collective-permute-start | bytes 245768 | tf_op jit(solution)/shard_map/ppermute | solution.py:167
  8.2 1.2 %copy-done = f32[1024,256]{1,0:T(8,128)S(1)} copy-done((f32[1024,256]{1,0:T(8,128)S(1)}, f32[1024,256]{1,0:T(8,128)}, u32[]{:S(2)}) %copy-start) | copy-done | bytes 1048600
  9.4 1.9 %shard_map.86 = (f32[256,512]{1,0:T(8,128)S(1)}, f32[1024,128]{1,0:T(8,128)S(1)}) custom-call(s32[1]{0:T(128)} %bitcast.core_ref, bf16[160,256]{1,0:T(8,128)(2,1)S(1)} %constant_dynamic-update-slice_fusion.block_ref.block_a, f32[1024,256]{1,0:T(8,128)S(1)} %copy-done), custom_call_target="tpu_custom_call" | custom-call | flops 1073741824 | bytes 3145728 | tf_op jit(solution)/shard_map/pallas_call | solution.py:143
  11.3 1.8 %collective-permute-done.block_ref.block_b = bf16[160,256]{1,0:T(8,128)(2,1)S(1)} collective-permute-done((bf16[160,256]{1,0:T(8,128)(2,1)S(1)}, bf16[160,256]{1,0:T(8,128)(2,1)S(1)}, u32[]{:S(2)}, u32[]{:S(2)}) %collective-permute-start) | collective-permute-done | bytes 81952 | tf_op jit(solution)/shard_map/ppermute | solution.py:167
  13.2 22.6 %all-gather = bf16[1024,256]{1,0:T(8,128)(2,1)S(1)} all-gather(bf16[256,256]{1,0:T(8,128)(2,1)S(1)} %pad_maximum_fusion), channel_id=2, replica_groups=mesh['yh'=2,'ym'=2,'yl'=2,'x'=4,'zl'=2,'zh'=4,'core'=2] {'zh'}, dimensions={0}, use_global_device_ids=true | all-gather | bytes 655360 | tf_op jit(solution)/shard_map/all_gather | solution.py:200
  35.8 1.9 %collective-permute-start.1 = (bf16[4,256,256]{2,1,0:T(8,128)(2,1)S(1)}, bf16[4,256,256]{2,1,0:T(8,128)(2,1)S(1)}, u32[]{:S(2)}, u32[]{:S(2)}) collective-permute-start(bf16[4,256,256]{2,1,0:T(8,128)(2,1)S(1)} %bitcast.24), channel_id=1, source_target_pairs={{0,1},{1,0},{2,3},{3,2},{4,5},{5,4},{6,7},{7,6},{8,9},{9,8},{10,11... | collective-permute-start | bytes 1572872 | tf_op jit(solution)/shard_map/ppermute | solution.py:167
  37.7 1.9 %shard_map.87 = (f32[256,512]{1,0:T(8,128)S(1)}, f32[1024,128]{1,0:T(8,128)S(1)}) custom-call(s32[1]{0:T(128)} %bitcast.core_ref, bf16[160,256]{1,0:T(8,128)(2,1)S(1)} %collective-permute-done.block_ref.block_b, f32[1024,256]{1,0:T(8,128)S(1)} %copy-done.1), custom_call_target="tpu_custom_call" | custom-call | flops 1073741824 | bytes 3145728 | tf_op jit(solution)/shard_map/pallas_call | solution.py:143
  39.7 5.0 %shard_map.88 = (bf16[4,128,256]{2,1,0:T(8,128)(2,1)S(1)}, bf16[4,128,256]{2,1,0:T(8,128)(2,1)S(1)}, bf16[16,64,256]{2,1,0:T(8,128)(2,1)}) custom-call(s32[1]{0:T(128)} %bitcast.core_ref, s32[1]{0:T(128)} %bitcast.1.zh_ref, bf16[160,256]{1,0:T(8,128)(2,1)S(1)} %constant_dynamic-update-slice_fusion.block_ref.block_a, ...), custom_call_target="tpu_custom_call" | custom-call | tf_op jit(solution)/shard_map/pallas_call | solution.py:156
  44.7 5.4 %all-to-all-start = ((bf16[16,64,256]{2,1,0:T(8,128)(2,1)}), bf16[16,64,256]{2,1,0:T(8,128)(2,1)S(1)}, u32[]{:S(2)}, u32[]{:S(2)}) async-start(bf16[16,64,256]{2,1,0:T(8,128)(2,1)} %get-tuple-element.24), calls=%async_computation | async-start | bytes 1048576 | tf_op jit(solution)/shard_map/all_to_all | solution.py:184
  50.2 2.1 %collective-permute-start.2 = (bf16[4,128,256]{2,1,0:T(8,128)(2,1)S(1)}, bf16[4,128,256]{2,1,0:T(8,128)(2,1)S(1)}, u32[]{:S(2)}, u32[]{:S(2)}) collective-permute-start(bf16[4,128,256]{2,1,0:T(8,128)(2,1)S(1)} %get-tuple-element.23), channel_id=1, source_target_pairs={{0,1},{1,0},{2,3},{3,2},{4,5},{5,4},{6,7},{7,6},{8,9},{9,8},{10,11... | collective-permute-start | bytes 786440 | tf_op jit(solution)/shard_map/ppermute | solution.py:167
  52.3 1.3 %collective-permute-done.2 = bf16[4,128,256]{2,1,0:T(8,128)(2,1)S(1)} collective-permute-done((bf16[4,128,256]{2,1,0:T(8,128)(2,1)S(1)}, bf16[4,128,256]{2,1,0:T(8,128)(2,1)S(1)}, u32[]{:S(2)}, u32[]{:S(2)}) %collective-permute-start.2) | collective-permute-done | bytes 262176 | tf_op jit(solution)/shard_map/ppermute | solution.py:167
  53.7 5.1 %collective-permute-start.3 = (f32[128,256]{1,0:T(8,128)S(1)}, f32[128,256]{1,0:T(8,128)S(1)}, u32[]{:S(2)}, u32[]{:S(2)}) collective-permute-start(f32[128,256]{1,0:T(8,128)S(1)} %slice_bitcast_fusion), channel_id=1, source_target_pairs={{0,4},{2,6},{4,0},{6,2},{1,5},{3,7},{5,1},{7,3},{8,12},{10,14},{12... | collective-permute-start | bytes 393224 | tf_op jit(solution)/shard_map/ppermute | solution.py:171
  58.8 2.1 %all-to-all-done = bf16[16,64,256]{2,1,0:T(8,128)(2,1)S(1)} async-done(((bf16[16,64,256]{2,1,0:T(8,128)(2,1)}), bf16[16,64,256]{2,1,0:T(8,128)(2,1)S(1)}, u32[]{:S(2)}, u32[]{:S(2)}) %all-to-all-start) | async-done | bytes 524320 | tf_op jit(solution)/shard_map/all_to_all | solution.py:184
  61.6 8.2 %all-to-all-start.1 = ((bf16[4,64,256]{2,1,0:T(8,128)(2,1)}), bf16[4,64,256]{2,1,0:T(8,128)(2,1)S(1)}, u32[]{:S(2)}, u32[]{:S(2)}) async-start(bf16[4,64,256]{2,1,0:T(8,128)(2,1)} %broadcast_in_dim.24), calls=%async_computation.1 | async-start | bytes 262144 | tf_op jit(solution)/shard_map/all_to_all | solution.py:176
  69.8 4.1 %collective-permute-start.4 = (bf16[128,256]{1,0:T(8,128)(2,1)S(1)}, bf16[128,256]{1,0:T(8,128)(2,1)S(1)}, u32[]{:S(2)}, u32[]{:S(2)}) collective-permute-start(bf16[128,256]{1,0:T(8,128)(2,1)S(1)} %get-tuple-element.31), channel_id=1, source_target_pairs={{0,2},{2,4},{4,6},{6,0},{1,3},{3,5},{5,7},{7,1},{8,10},{10,12},{12... | collective-permute-start | bytes 196616 | tf_op jit(solution)/shard_map/ppermute | solution.py:171
  73.9 4.6 %collective-permute-done.4 = bf16[128,256]{1,0:T(8,128)(2,1)S(1)} collective-permute-done((bf16[128,256]{1,0:T(8,128)(2,1)S(1)}, bf16[128,256]{1,0:T(8,128)(2,1)S(1)}, u32[]{:S(2)}, u32[]{:S(2)}) %collective-permute-start.4) | collective-permute-done | bytes 65568 | tf_op jit(solution)/shard_map/ppermute | solution.py:171
  78.5 0.8 broadcast_in_dim.25
  79.3 4.9 %all-to-all-start.2 = ((bf16[16,64,256]{2,1,0:T(8,128)(2,1)}), bf16[16,64,256]{2,1,0:T(8,128)(2,1)S(1)}, u32[]{:S(2)}, u32[]{:S(2)}) async-start(bf16[16,64,256]{2,1,0:T(8,128)(2,1)} %broadcast_in_dim.25), calls=%async_computation.2 | async-start | bytes 1048576 | tf_op jit(solution)/shard_map/all_to_all | solution.py:176
  84.2 3.1 %collective-permute-start.5 = (bf16[128,256]{1,0:T(8,128)(2,1)S(1)}, bf16[128,256]{1,0:T(8,128)(2,1)S(1)}, u32[]{:S(2)}, u32[]{:S(2)}) collective-permute-start(bf16[128,256]{1,0:T(8,128)(2,1)S(1)} %get-tuple-element.30), channel_id=1, source_target_pairs={{0,6},{2,0},{4,2},{6,4},{1,7},{3,1},{5,3},{7,5},{8,14},{10,8},{12,... | collective-permute-start | bytes 196616 | tf_op jit(solution)/shard_map/ppermute | solution.py:171
  87.3 4.7 %collective-permute-done.5 = bf16[128,256]{1,0:T(8,128)(2,1)S(1)} collective-permute-done((bf16[128,256]{1,0:T(8,128)(2,1)S(1)}, bf16[128,256]{1,0:T(8,128)(2,1)S(1)}, u32[]{:S(2)}, u32[]{:S(2)}) %collective-permute-start.5) | collective-permute-done | bytes 65568 | tf_op jit(solution)/shard_map/ppermute | solution.py:171
  92.1 0.7 fusion.2
  92.7 2.4 %all-to-all-done.2 = bf16[16,64,256]{2,1,0:T(8,128)(2,1)S(1)} async-done(((bf16[16,64,256]{2,1,0:T(8,128)(2,1)}), bf16[16,64,256]{2,1,0:T(8,128)(2,1)S(1)}, u32[]{:S(2)}, u32[]{:S(2)}) %all-to-all-start.2) | async-done | bytes 524320 | tf_op jit(solution)/shard_map/all_to_all | solution.py:176
  95.1 1.1 %bitcast_convert_fusion = f32[1024,256]{1,0:T(8,128)} fusion(bf16[16,64,256]{2,1,0:T(8,128)(2,1)S(1)} %all-to-all-done.2), kind=kLoop, calls=%fused_computation | loop fusion | flops 262144 | bytes 1572864 | tf_op jit(solution)/shard_map/convert_element_type | solution.py:215
  (25 shorter events, 0.9 us)
Async XLA Ops:
  0.6 0.7 copy-start.3
  0.6 1.5 %copy-start.2 = (bf16[128,256]{1,0:T(8,128)(2,1)S(1)}, bf16[128,256]{1,0:T(8,128)(2,1)}, u32[]{:S(2)}) copy-start(bf16[128,256]{1,0:T(8,128)(2,1)} %param.7) | copy-start | bytes 196612
  2.2 10.9 %collective-permute-start = (bf16[160,256]{1,0:T(8,128)(2,1)S(1)}, bf16[160,256]{1,0:T(8,128)(2,1)S(1)}, u32[]{:S(2)}, u32[]{:S(2)}) collective-permute-start(bf16[160,256]{1,0:T(8,128)(2,1)S(1)} %constant_dynamic-update-slice_fusion.block_ref.block_a), channel_id=1, source_target_pairs={{0,256},{256,0},{1,257},{257,1},{2,258},{258,2},{3,259},{259,3},{4... | collective-permute-start | bytes 245768 | tf_op jit(solution)/shard_map/ppermute | solution.py:167
  8.2 1.2 %copy-start = (f32[1024,256]{1,0:T(8,128)S(1)}, f32[1024,256]{1,0:T(8,128)}, u32[]{:S(2)}) copy-start(f32[1024,256]{1,0:T(8,128)} %table_ref.3) | copy-start | bytes 3145732
  11.3 26.4 %copy-start.1 = (f32[1024,256]{1,0:T(8,128)S(1)}, f32[1024,256]{1,0:T(8,128)}, u32[]{:S(2)}) copy-start(f32[1024,256]{1,0:T(8,128)} %table_ref.3) | copy-start | bytes 3145732
  35.8 3.9 %collective-permute-start.1 = (bf16[4,256,256]{2,1,0:T(8,128)(2,1)S(1)}, bf16[4,256,256]{2,1,0:T(8,128)(2,1)S(1)}, u32[]{:S(2)}, u32[]{:S(2)}) collective-permute-start(bf16[4,256,256]{2,1,0:T(8,128)(2,1)S(1)} %bitcast.24), channel_id=1, source_target_pairs={{0,1},{1,0},{2,3},{3,2},{4,5},{5,4},{6,7},{7,6},{8,9},{9,8},{10,11... | collective-permute-start | bytes 1572872 | tf_op jit(solution)/shard_map/ppermute | solution.py:167
  44.7 16.2 %all-to-all-start = ((bf16[16,64,256]{2,1,0:T(8,128)(2,1)}), bf16[16,64,256]{2,1,0:T(8,128)(2,1)S(1)}, u32[]{:S(2)}, u32[]{:S(2)}) async-start(bf16[16,64,256]{2,1,0:T(8,128)(2,1)} %get-tuple-element.24), calls=%async_computation | async-start | bytes 1048576 | tf_op jit(solution)/shard_map/all_to_all | solution.py:184
  50.2 3.4 %collective-permute-start.2 = (bf16[4,128,256]{2,1,0:T(8,128)(2,1)S(1)}, bf16[4,128,256]{2,1,0:T(8,128)(2,1)S(1)}, u32[]{:S(2)}, u32[]{:S(2)}) collective-permute-start(bf16[4,128,256]{2,1,0:T(8,128)(2,1)S(1)} %get-tuple-element.23), channel_id=1, source_target_pairs={{0,1},{1,0},{2,3},{3,2},{4,5},{5,4},{6,7},{7,6},{8,9},{9,8},{10,11... | collective-permute-start | bytes 786440 | tf_op jit(solution)/shard_map/ppermute | solution.py:167
  53.7 24.8 %collective-permute-start.3 = (f32[128,256]{1,0:T(8,128)S(1)}, f32[128,256]{1,0:T(8,128)S(1)}, u32[]{:S(2)}, u32[]{:S(2)}) collective-permute-start(f32[128,256]{1,0:T(8,128)S(1)} %slice_bitcast_fusion), channel_id=1, source_target_pairs={{0,4},{2,6},{4,0},{6,2},{1,5},{3,7},{5,1},{7,3},{8,12},{10,14},{12... | collective-permute-start | bytes 393224 | tf_op jit(solution)/shard_map/ppermute | solution.py:171
  61.6 16.8 %all-to-all-start.1 = ((bf16[4,64,256]{2,1,0:T(8,128)(2,1)}), bf16[4,64,256]{2,1,0:T(8,128)(2,1)S(1)}, u32[]{:S(2)}, u32[]{:S(2)}) async-start(bf16[4,64,256]{2,1,0:T(8,128)(2,1)} %broadcast_in_dim.24), calls=%async_computation.1 | async-start | bytes 262144 | tf_op jit(solution)/shard_map/all_to_all | solution.py:176
  69.8 8.6 %collective-permute-start.4 = (bf16[128,256]{1,0:T(8,128)(2,1)S(1)}, bf16[128,256]{1,0:T(8,128)(2,1)S(1)}, u32[]{:S(2)}, u32[]{:S(2)}) collective-permute-start(bf16[128,256]{1,0:T(8,128)(2,1)S(1)} %get-tuple-element.31), channel_id=1, source_target_pairs={{0,2},{2,4},{4,6},{6,0},{1,3},{3,5},{5,7},{7,1},{8,10},{10,12},{12... | collective-permute-start | bytes 196616 | tf_op jit(solution)/shard_map/ppermute | solution.py:171
  79.3 15.8 %all-to-all-start.2 = ((bf16[16,64,256]{2,1,0:T(8,128)(2,1)}), bf16[16,64,256]{2,1,0:T(8,128)(2,1)S(1)}, u32[]{:S(2)}, u32[]{:S(2)}) async-start(bf16[16,64,256]{2,1,0:T(8,128)(2,1)} %broadcast_in_dim.25), calls=%async_computation.2 | async-start | bytes 1048576 | tf_op jit(solution)/shard_map/all_to_all | solution.py:176
  84.2 7.8 %collective-permute-start.5 = (bf16[128,256]{1,0:T(8,128)(2,1)S(1)}, bf16[128,256]{1,0:T(8,128)(2,1)S(1)}, u32[]{:S(2)}, u32[]{:S(2)}) collective-permute-start(bf16[128,256]{1,0:T(8,128)(2,1)S(1)} %get-tuple-element.30), channel_id=1, source_target_pairs={{0,6},{2,0},{4,2},{6,4},{1,7},{3,1},{5,3},{7,5},{8,14},{10,8},{12,... | collective-permute-start | bytes 196616 | tf_op jit(solution)/shard_map/ppermute | solution.py:171

commit v5 on v4

--- a/solution.py
+++ b/solution.py
@@ -110,8 +110,8 @@
         scores = dot(tails, query, 1, 0)
         often = counts_ref[step * CHUNK:(step + 1) * CHUNK, :]
         often = jnp.concatenate([often] * (EDGES // 128), axis=1)
-        both = (0.5 * jnp.tanh(0.5 * scores) + 0.5) * often * alive
-        return (both + jnp.where(rows == rhs - step * CHUNK, pos_grad, 0.0)).astype(BF16)
+        both = (jnp.tanh(0.5 * scores) + 1.0) * (often * (0.5 * alive))
+        return jnp.where(rows == rhs - step * CHUNK, both + pos_grad, both).astype(BF16)
 
     lhs, rhs, alive, h, query, pos_grad = queries(pack_a, w_a, 0)
     grad = jnp.zeros((D, EDGES), F32)
@@ -130,7 +130,7 @@
         both = score_grads(chunk_of(0, step), query, counts_b, step, rhs, alive, pos_grad)
         out = (dot(both, query, 1, 1) + dot(one_hot(lhs, step), head, 1, 1)).astype(BF16)
         for half in range(2):
-            d = jnp.bitwise_and(2 * (step % 2) + half - zh, 3)
+            d = jnp.bitwise_xor(2 * (step % 2) + half, zh)
             ref = mine_out if step < 2 else other_out
             ref[d] = out[half * SHARD:(half + 1) * SHARD]
         out = dot(one_hot(rel, step), term, 1, 1).astype(BF16)
@@ -165,10 +165,6 @@
 def swap(block, axis, distance=1):
     size = lax.axis_size(axis)
     return lax.ppermute(block, axis, [(i, i ^ distance) for i in range(size)])
-
-
-def move(block, step):
-    return lax.ppermute(block, "zh", [(i, (i + step) % 4) for i in range(4)])
 
 
 def spread(block, axis, size):
@@ -206,11 +202,12 @@
     from_core = swap(other_sum, "core")
     parts = exchange(rel_part, NEAR)
     chip = mine_sum.astype(F32) + from_core.astype(F32)
-    two = move(chip[2], 2)
-    one, three = move(chip[1].astype(BF16), 1), move(chip[3].astype(BF16), 3)
+    far = swap(chip[2:], "zh", 2)
     parts = spread(summed(parts), FAR, 4)
-    two, one, parts = tie(two, one, parts)
-    shard = chip[0] + two + one.astype(F32) + three.astype(F32)
+    far, parts = tie(far, parts)
+    pair = chip[:2] + far
+    near = swap(pair[1].astype(BF16), "zh", 1)
+    shard = pair[0] + near.astype(F32)
     rel_all = spread(summed(parts), NEAR, 16).reshape(PARTS, D)
     return shard, rel_all.astype(F32)
 

time: 96.9 us -> 94.7 us (0.977)
  the two profiles are of different devices: /device:TPU:16 before, /device:TPU:120 now
where the time goes in v5:
time: 94.7 us; the launch traced here: 94.1 us
  starting transfers between devices  40.9 us (43%)
  blocking collectives  21 us (22%)
  waiting for transfers between devices  16.4 us (17%)
  Pallas kernels  8.76 us (9%)
  local copies, waits for them, and re-layouts  3.61 us (4%)
  other arithmetic  1.95 us (2%)
  between operations  1.49 us (2%)
    all_gather x1, blocking collectives, local(): mine = lax.all_gather(both, 'zh', axis=0, tiled=False)  21 us
    ppermute x5, starting transfers between devices, swap(): return lax.ppermute(block, axis, [(i, i ^ distance) for i in range(size)])  20.1 us
    all_to_all x2, starting transfers between devices, spread(): return lax.all_to_all(copies, axis, 0, 0)  13.9 us
    ppermute x5, waiting for transfers between devices, swap(): return lax.ppermute(block, axis, [(i, i ^ distance) for i in range(size)])  11.3 us
    all_to_all x1, starting transfers between devices, exchange(): return lax.all_to_all(blocks, axis, 0, 0)  6.99 us
    pallas_call x1, Pallas kernels, edge_terms(): pl.pallas_call(edge_kernel, out_shape=(block, block, jax.ShapeDtypeStruct...  4.89 us
    all_to_all x2, waiting for transfers between devices, spread(): return lax.all_to_all(copies, axis, 0, 0)  4.58 us
    pallas_call x2, Pallas kernels, early_terms(): pl.pallas_call(early_kernel, out_shape=(jax.ShapeDtypeStruct((D, EDGES),...  3.87 us
  transfers between devices with their start and end apart: 8, of which 6 were waited for; matrix products, arithmetic and copies ran while one was open for 2% of the time, Pallas kernels for 4%

profile of v5, /device:TPU:120, one launch (start us, length us, event | category | flops | bytes accessed | tf_op | source)
XLA Modules:
  0.0 94.1 jit_solution(2117098334419726486)
XLA Ops:
  1.3 0.8 concatenate.12
  2.2 4.7 %collective-permute-start = (bf16[160,256]{1,0:T(8,128)(2,1)S(1)}, bf16[160,256]{1,0:T(8,128)(2,1)S(1)}, u32[]{:S(2)}, u32[]{:S(2)}) collective-permute-start(bf16[160,256]{1,0:T(8,128)(2,1)S(1)} %constant_dynamic-update-slice_fusion.block_ref.block_a), channel_id=1, source_target_pairs={{0,256},{256,0},{1,257},{257,1},{2,258},{258,2},{3,259},{259,3},{4... | collective-permute-start | bytes 245768 | tf_op jit(solution)/shard_map/ppermute | solution.py:167
  7.0 1.2 %copy-done = f32[1024,256]{1,0:T(8,128)S(1)} copy-done((f32[1024,256]{1,0:T(8,128)S(1)}, f32[1024,256]{1,0:T(8,128)}, u32[]{:S(2)}) %copy-start) | copy-done | bytes 1048600
  8.2 1.9 %shard_map.86 = (f32[256,512]{1,0:T(8,128)S(1)}, f32[1024,128]{1,0:T(8,128)S(1)}) custom-call(s32[1]{0:T(128)} %bitcast.core_ref, bf16[160,256]{1,0:T(8,128)(2,1)S(1)} %constant_dynamic-update-slice_fusion.block_ref.block_a, f32[1024,256]{1,0:T(8,128)S(1)} %copy-done), custom_call_target="tpu_custom_call" | custom-call | flops 1073741824 | bytes 3145728 | tf_op jit(solution)/shard_map/pallas_call | solution.py:143
  10.1 3.9 %collective-permute-done.block_ref.block_b = bf16[160,256]{1,0:T(8,128)(2,1)S(1)} collective-permute-done((bf16[160,256]{1,0:T(8,128)(2,1)S(1)}, bf16[160,256]{1,0:T(8,128)(2,1)S(1)}, u32[]{:S(2)}, u32[]{:S(2)}) %collective-permute-start) | collective-permute-done | bytes 81952 | tf_op jit(solution)/shard_map/ppermute | solution.py:167
  14.0 21.0 %all-gather = bf16[1024,256]{1,0:T(8,128)(2,1)S(1)} all-gather(bf16[256,256]{1,0:T(8,128)(2,1)S(1)} %pad_maximum_fusion), channel_id=2, replica_groups=mesh['yh'=2,'ym'=2,'yl'=2,'x'=4,'zl'=2,'zh'=4,'core'=2] {'zh'}, dimensions={0}, use_global_device_ids=true | all-gather | bytes 655360 | tf_op jit(solution)/shard_map/all_gather | solution.py:196
  34.9 1.9 %collective-permute-start.1 = (bf16[4,256,256]{2,1,0:T(8,128)(2,1)S(1)}, bf16[4,256,256]{2,1,0:T(8,128)(2,1)S(1)}, u32[]{:S(2)}, u32[]{:S(2)}) collective-permute-start(bf16[4,256,256]{2,1,0:T(8,128)(2,1)S(1)} %bitcast.16), channel_id=1, source_target_pairs={{0,1},{1,0},{2,3},{3,2},{4,5},{5,4},{6,7},{7,6},{8,9},{9,8},{10,11... | collective-permute-start | bytes 1572872 | tf_op jit(solution)/shard_map/ppermute | solution.py:167
  36.9 1.9 %shard_map.87 = (f32[256,512]{1,0:T(8,128)S(1)}, f32[1024,128]{1,0:T(8,128)S(1)}) custom-call(s32[1]{0:T(128)} %bitcast.core_ref, bf16[160,256]{1,0:T(8,128)(2,1)S(1)} %collective-permute-done.block_ref.block_b, f32[1024,256]{1,0:T(8,128)S(1)} %copy-done.1), custom_call_target="tpu_custom_call" | custom-call | flops 1073741824 | bytes 3145728 | tf_op jit(solution)/shard_map/pallas_call | solution.py:143
  38.8 4.9 %shard_map.88 = (bf16[4,128,256]{2,1,0:T(8,128)(2,1)S(1)}, bf16[4,128,256]{2,1,0:T(8,128)(2,1)S(1)}, bf16[16,64,256]{2,1,0:T(8,128)(2,1)}) custom-call(s32[1]{0:T(128)} %bitcast.core_ref, s32[1]{0:T(128)} %bitcast.1.zh_ref, bf16[160,256]{1,0:T(8,128)(2,1)S(1)} %constant_dynamic-update-slice_fusion.block_ref.block_a, ...), custom_call_target="tpu_custom_call" | custom-call | tf_op jit(solution)/shard_map/pallas_call | solution.py:156
  43.7 7.0 %all-to-all-start = ((bf16[16,64,256]{2,1,0:T(8,128)(2,1)}), bf16[16,64,256]{2,1,0:T(8,128)(2,1)S(1)}, u32[]{:S(2)}, u32[]{:S(2)}) async-start(bf16[16,64,256]{2,1,0:T(8,128)(2,1)} %get-tuple-element.23), calls=%async_computation | async-start | bytes 1048576 | tf_op jit(solution)/shard_map/all_to_all | solution.py:180
  50.7 1.9 %collective-permute-start.2 = (bf16[4,128,256]{2,1,0:T(8,128)(2,1)S(1)}, bf16[4,128,256]{2,1,0:T(8,128)(2,1)S(1)}, u32[]{:S(2)}, u32[]{:S(2)}) collective-permute-start(bf16[4,128,256]{2,1,0:T(8,128)(2,1)S(1)} %get-tuple-element.22), channel_id=1, source_target_pairs={{0,1},{1,0},{2,3},{3,2},{4,5},{5,4},{6,7},{7,6},{8,9},{9,8},{10,11... | collective-permute-start | bytes 786440 | tf_op jit(solution)/shard_map/ppermute | solution.py:167
  52.6 1.5 %collective-permute-done.2 = bf16[4,128,256]{2,1,0:T(8,128)(2,1)S(1)} collective-permute-done((bf16[4,128,256]{2,1,0:T(8,128)(2,1)S(1)}, bf16[4,128,256]{2,1,0:T(8,128)(2,1)S(1)}, u32[]{:S(2)}, u32[]{:S(2)}) %collective-permute-start.2) | collective-permute-done | bytes 262176 | tf_op jit(solution)/shard_map/ppermute | solution.py:167
  54.2 5.2 %collective-permute-start.3 = (f32[2,128,256]{2,1,0:T(8,128)S(1)}, f32[2,128,256]{2,1,0:T(8,128)S(1)}, u32[]{:S(2)}, u32[]{:S(2)}) collective-permute-start(f32[2,128,256]{2,1,0:T(8,128)S(1)} %slice.22), channel_id=1, source_target_pairs={{0,4},{2,6},{4,0},{6,2},{1,5},{3,7},{5,1},{7,3},{8,12},{10,14},{12... | collective-permute-start | bytes 786440 | tf_op jit(solution)/shard_map/ppermute | solution.py:167
  59.4 0.6 all-to-all-done
  60.1 0.7 broadcast_in_dim.24
  60.8 7.4 %all-to-all-start.1 = ((bf16[4,64,256]{2,1,0:T(8,128)(2,1)}), bf16[4,64,256]{2,1,0:T(8,128)(2,1)S(1)}, u32[]{:S(2)}, u32[]{:S(2)}) async-start(bf16[4,64,256]{2,1,0:T(8,128)(2,1)} %broadcast_in_dim.24), calls=%async_computation.1 | async-start | bytes 262144 | tf_op jit(solution)/shard_map/all_to_all | solution.py:172
  68.1 0.3 collective-permute-done.3
  68.5 4.6 %all-to-all-done.1 = bf16[4,64,256]{2,1,0:T(8,128)(2,1)S(1)} async-done(((bf16[4,64,256]{2,1,0:T(8,128)(2,1)}), bf16[4,64,256]{2,1,0:T(8,128)(2,1)S(1)}, u32[]{:S(2)}, u32[]{:S(2)}) %all-to-all-start.1) | async-done | bytes 131104 | tf_op jit(solution)/shard_map/all_to_all | solution.py:172
  73.1 0.8 broadcast_in_dim.25
  73.9 6.5 %all-to-all-start.2 = ((bf16[16,64,256]{2,1,0:T(8,128)(2,1)}), bf16[16,64,256]{2,1,0:T(8,128)(2,1)S(1)}, u32[]{:S(2)}, u32[]{:S(2)}) async-start(bf16[16,64,256]{2,1,0:T(8,128)(2,1)} %broadcast_in_dim.25), calls=%async_computation.2 | async-start | bytes 1048576 | tf_op jit(solution)/shard_map/all_to_all | solution.py:172
  80.4 6.3 %collective-permute-start.4 = (bf16[128,256]{1,0:T(8,128)(2,1)S(1)}, bf16[128,256]{1,0:T(8,128)(2,1)S(1)}, u32[]{:S(2)}, u32[]{:S(2)}) collective-permute-start(bf16[128,256]{1,0:T(8,128)(2,1)S(1)} %fusion.1), channel_id=1, source_target_pairs={{0,2},{2,0},{4,6},{6,4},{1,3},{3,1},{5,7},{7,5},{8,10},{10,8},{12,... | collective-permute-start | bytes 196616 | tf_op jit(solution)/shard_map/ppermute | solution.py:167
  86.7 5.6 %collective-permute-done.4 = bf16[128,256]{1,0:T(8,128)(2,1)S(1)} collective-permute-done((bf16[128,256]{1,0:T(8,128)(2,1)S(1)}, bf16[128,256]{1,0:T(8,128)(2,1)S(1)}, u32[]{:S(2)}, u32[]{:S(2)}) %collective-permute-start.4) | collective-permute-done | bytes 65568 | tf_op jit(solution)/shard_map/ppermute | solution.py:167
  92.3 0.7 fusion
  93.0 1.1 %bitcast_convert_fusion = f32[1024,256]{1,0:T(8,128)} fusion(bf16[16,64,256]{2,1,0:T(8,128)(2,1)S(1)} %all-to-all-done.2), kind=kLoop, calls=%fused_computation | loop fusion | flops 262144 | bytes 1572864 | tf_op jit(solution)/shard_map/convert_element_type | solution.py:212
  (24 shorter events, 0.3 us)
Async XLA Ops:
  0.6 0.7 copy-start.3
  0.6 1.5 %copy-start.2 = (bf16[128,256]{1,0:T(8,128)(2,1)S(1)}, bf16[128,256]{1,0:T(8,128)(2,1)}, u32[]{:S(2)}) copy-start(bf16[128,256]{1,0:T(8,128)(2,1)} %param.7) | copy-start | bytes 196612
  2.2 11.7 %collective-permute-start = (bf16[160,256]{1,0:T(8,128)(2,1)S(1)}, bf16[160,256]{1,0:T(8,128)(2,1)S(1)}, u32[]{:S(2)}, u32[]{:S(2)}) collective-permute-start(bf16[160,256]{1,0:T(8,128)(2,1)S(1)} %constant_dynamic-update-slice_fusion.block_ref.block_a), channel_id=1, source_target_pairs={{0,256},{256,0},{1,257},{257,1},{2,258},{258,2},{3,259},{259,3},{4... | collective-permute-start | bytes 245768 | tf_op jit(solution)/shard_map/ppermute | solution.py:167
  7.0 1.2 %copy-start = (f32[1024,256]{1,0:T(8,128)S(1)}, f32[1024,256]{1,0:T(8,128)}, u32[]{:S(2)}) copy-start(f32[1024,256]{1,0:T(8,128)} %table_ref.3) | copy-start | bytes 3145732
  10.1 26.8 %copy-start.1 = (f32[1024,256]{1,0:T(8,128)S(1)}, f32[1024,256]{1,0:T(8,128)}, u32[]{:S(2)}) copy-start(f32[1024,256]{1,0:T(8,128)} %table_ref.3) | copy-start | bytes 3145732
  34.9 3.9 %collective-permute-start.1 = (bf16[4,256,256]{2,1,0:T(8,128)(2,1)S(1)}, bf16[4,256,256]{2,1,0:T(8,128)(2,1)S(1)}, u32[]{:S(2)}, u32[]{:S(2)}) collective-permute-start(bf16[4,256,256]{2,1,0:T(8,128)(2,1)S(1)} %bitcast.16), channel_id=1, source_target_pairs={{0,1},{1,0},{2,3},{3,2},{4,5},{5,4},{6,7},{7,6},{8,9},{9,8},{10,11... | collective-permute-start | bytes 1572872 | tf_op jit(solution)/shard_map/ppermute | solution.py:167
  43.7 16.3 %all-to-all-start = ((bf16[16,64,256]{2,1,0:T(8,128)(2,1)}), bf16[16,64,256]{2,1,0:T(8,128)(2,1)S(1)}, u32[]{:S(2)}, u32[]{:S(2)}) async-start(bf16[16,64,256]{2,1,0:T(8,128)(2,1)} %get-tuple-element.23), calls=%async_computation | async-start | bytes 1048576 | tf_op jit(solution)/shard_map/all_to_all | solution.py:180
  50.7 3.4 %collective-permute-start.2 = (bf16[4,128,256]{2,1,0:T(8,128)(2,1)S(1)}, bf16[4,128,256]{2,1,0:T(8,128)(2,1)S(1)}, u32[]{:S(2)}, u32[]{:S(2)}) collective-permute-start(bf16[4,128,256]{2,1,0:T(8,128)(2,1)S(1)} %get-tuple-element.22), channel_id=1, source_target_pairs={{0,1},{1,0},{2,3},{3,2},{4,5},{5,4},{6,7},{7,6},{8,9},{9,8},{10,11... | collective-permute-start | bytes 786440 | tf_op jit(solution)/shard_map/ppermute | solution.py:167
  54.2 14.3 %collective-permute-start.3 = (f32[2,128,256]{2,1,0:T(8,128)S(1)}, f32[2,128,256]{2,1,0:T(8,128)S(1)}, u32[]{:S(2)}, u32[]{:S(2)}) collective-permute-start(f32[2,128,256]{2,1,0:T(8,128)S(1)} %slice.22), channel_id=1, source_target_pairs={{0,4},{2,6},{4,0},{6,2},{1,5},{3,7},{5,1},{7,3},{8,12},{10,14},{12... | collective-permute-start | bytes 786440 | tf_op jit(solution)/shard_map/ppermute | solution.py:167
  60.8 12.3 %all-to-all-start.1 = ((bf16[4,64,256]{2,1,0:T(8,128)(2,1)}), bf16[4,64,256]{2,1,0:T(8,128)(2,1)S(1)}, u32[]{:S(2)}, u32[]{:S(2)}) async-start(bf16[4,64,256]{2,1,0:T(8,128)(2,1)} %broadcast_in_dim.24), calls=%async_computation.1 | async-start | bytes 262144 | tf_op jit(solution)/shard_map/all_to_all | solution.py:172
  73.9 19.1 %all-to-all-start.2 = ((bf16[16,64,256]{2,1,0:T(8,128)(2,1)}), bf16[16,64,256]{2,1,0:T(8,128)(2,1)S(1)}, u32[]{:S(2)}, u32[]{:S(2)}) async-start(bf16[16,64,256]{2,1,0:T(8,128)(2,1)} %broadcast_in_dim.25), calls=%async_computation.2 | async-start | bytes 1048576 | tf_op jit(solution)/shard_map/all_to_all | solution.py:172
  80.4 11.9 %collective-permute-start.4 = (bf16[128,256]{1,0:T(8,128)(2,1)S(1)}, bf16[128,256]{1,0:T(8,128)(2,1)S(1)}, u32[]{:S(2)}, u32[]{:S(2)}) collective-permute-start(bf16[128,256]{1,0:T(8,128)(2,1)S(1)} %fusion.1), channel_id=1, source_target_pairs={{0,2},{2,0},{4,6},{6,4},{1,3},{3,1},{5,7},{7,5},{8,10},{10,8},{12,... | collective-permute-start | bytes 196616 | tf_op jit(solution)/shard_map/ppermute | solution.py:167

commit v6 on v5

--- a/solution.py
+++ b/solution.py
@@ -207,9 +207,9 @@
     far, parts = tie(far, parts)
     pair = chip[:2] + far
     near = swap(pair[1].astype(BF16), "zh", 1)
-    shard = pair[0] + near.astype(F32)
-    rel_all = spread(summed(parts), NEAR, 16).reshape(PARTS, D)
-    return shard, rel_all.astype(F32)
+    rel_all = spread(summed(parts), NEAR, 16).reshape(PARTS, D).astype(F32)
+    near, rel_all = tie(near, rel_all)
+    return pair[0] + near.astype(F32), rel_all
 
 
 def solution(mesh):

time: 94.7 us -> 95.2 us (level)
  the two profiles are of different devices: /device:TPU:120 before, /device:TPU:2 now
where the time goes in v6:
time: 95.2 us; the launch traced here: 94.5 us
  starting transfers between devices  40.6 us (43%)
  blocking collectives  21.2 us (22%)
  waiting for transfers between devices  16.9 us (18%)
  Pallas kernels  8.76 us (9%)
  local copies, waits for them, and re-layouts  3.61 us (4%)
  other arithmetic  1.95 us (2%)
  between operations  1.49 us (2%)
    all_gather x1, blocking collectives, local(): mine = lax.all_gather(both, 'zh', axis=0, tiled=False)  21.2 us
    ppermute x5, starting transfers between devices, swap(): return lax.ppermute(block, axis, [(i, i ^ distance) for i in range(size)])  20.4 us
    all_to_all x2, waiting for transfers between devices, spread(): return lax.all_to_all(copies, axis, 0, 0)  13.9 us
    all_to_all x2, starting transfers between devices, spread(): return lax.all_to_all(copies, axis, 0, 0)  13.1 us
    all_to_all x1, starting transfers between devices, exchange(): return lax.all_to_all(blocks, axis, 0, 0)  7.05 us
    pallas_call x1, Pallas kernels, edge_terms(): pl.pallas_call(edge_kernel, out_shape=(block, block, jax.ShapeDtypeStruct...  4.9 us
    pallas_call x2, Pallas kernels, early_terms(): pl.pallas_call(early_kernel, out_shape=(jax.ShapeDtypeStruct((D, EDGES),...  3.86 us
    ppermute x5, waiting for transfers between devices, swap(): return lax.ppermute(block, axis, [(i, i ^ distance) for i in range(size)])  2.32 us
  transfers between devices with their start and end apart: 8, of which 6 were waited for; matrix products, arithmetic and copies ran while one was open for 2% of the time, Pallas kernels for 4%

profile of v6, /device:TPU:2, one launch (start us, length us, event | category | flops | bytes accessed | tf_op | source)
XLA Modules:
  0.0 94.5 jit_solution(15540233874519720504)
XLA Ops:
  1.3 0.8 concatenate.12
  2.2 7.7 %collective-permute-start = (bf16[160,256]{1,0:T(8,128)(2,1)S(1)}, bf16[160,256]{1,0:T(8,128)(2,1)S(1)}, u32[]{:S(2)}, u32[]{:S(2)}) collective-permute-start(bf16[160,256]{1,0:T(8,128)(2,1)S(1)} %constant_dynamic-update-slice_fusion.block_ref.block_a), channel_id=1, source_target_pairs={{0,256},{256,0},{1,257},{257,1},{2,258},{258,2},{3,259},{259,3},{4... | collective-permute-start | bytes 245768 | tf_op jit(solution)/shard_map/ppermute | solution.py:167
  10.0 1.2 %copy-done = f32[1024,256]{1,0:T(8,128)S(1)} copy-done((f32[1024,256]{1,0:T(8,128)S(1)}, f32[1024,256]{1,0:T(8,128)}, u32[]{:S(2)}) %copy-start) | copy-done | bytes 1048600
  11.2 1.9 %shard_map.86 = (f32[256,512]{1,0:T(8,128)S(1)}, f32[1024,128]{1,0:T(8,128)S(1)}) custom-call(s32[1]{0:T(128)} %bitcast.core_ref, bf16[160,256]{1,0:T(8,128)(2,1)S(1)} %constant_dynamic-update-slice_fusion.block_ref.block_a, f32[1024,256]{1,0:T(8,128)S(1)} %copy-done), custom_call_target="tpu_custom_call" | custom-call | flops 1073741824 | bytes 3145728 | tf_op jit(solution)/shard_map/pallas_call | solution.py:143
  13.1 0.5 collective-permute-done.block_ref.block_b
  13.6 21.2 %all-gather = bf16[1024,256]{1,0:T(8,128)(2,1)S(1)} all-gather(bf16[256,256]{1,0:T(8,128)(2,1)S(1)} %pad_maximum_fusion), channel_id=2, replica_groups=mesh['yh'=2,'ym'=2,'yl'=2,'x'=4,'zl'=2,'zh'=4,'core'=2] {'zh'}, dimensions={0}, use_global_device_ids=true | all-gather | bytes 655360 | tf_op jit(solution)/shard_map/all_gather | solution.py:196
  34.8 1.9 %collective-permute-start.1 = (bf16[4,256,256]{2,1,0:T(8,128)(2,1)S(1)}, bf16[4,256,256]{2,1,0:T(8,128)(2,1)S(1)}, u32[]{:S(2)}, u32[]{:S(2)}) collective-permute-start(bf16[4,256,256]{2,1,0:T(8,128)(2,1)S(1)} %bitcast.16), channel_id=1, source_target_pairs={{0,1},{1,0},{2,3},{3,2},{4,5},{5,4},{6,7},{7,6},{8,9},{9,8},{10,11... | collective-permute-start | bytes 1572872 | tf_op jit(solution)/shard_map/ppermute | solution.py:167
  36.7 1.9 %shard_map.87 = (f32[256,512]{1,0:T(8,128)S(1)}, f32[1024,128]{1,0:T(8,128)S(1)}) custom-call(s32[1]{0:T(128)} %bitcast.core_ref, bf16[160,256]{1,0:T(8,128)(2,1)S(1)} %collective-permute-done.block_ref.block_b, f32[1024,256]{1,0:T(8,128)S(1)} %copy-done.1), custom_call_target="tpu_custom_call" | custom-call | flops 1073741824 | bytes 3145728 | tf_op jit(solution)/shard_map/pallas_call | solution.py:143
  38.7 4.9 %shard_map.88 = (bf16[4,128,256]{2,1,0:T(8,128)(2,1)S(1)}, bf16[4,128,256]{2,1,0:T(8,128)(2,1)S(1)}, bf16[16,64,256]{2,1,0:T(8,128)(2,1)}) custom-call(s32[1]{0:T(128)} %bitcast.core_ref, s32[1]{0:T(128)} %bitcast.1.zh_ref, bf16[160,256]{1,0:T(8,128)(2,1)S(1)} %constant_dynamic-update-slice_fusion.block_ref.block_a, ...), custom_call_target="tpu_custom_call" | custom-call | tf_op jit(solution)/shard_map/pallas_call | solution.py:156
  43.6 7.0 %all-to-all-start = ((bf16[16,64,256]{2,1,0:T(8,128)(2,1)}), bf16[16,64,256]{2,1,0:T(8,128)(2,1)S(1)}, u32[]{:S(2)}, u32[]{:S(2)}) async-start(bf16[16,64,256]{2,1,0:T(8,128)(2,1)} %get-tuple-element.25), calls=%async_computation | async-start | bytes 1048576 | tf_op jit(solution)/shard_map/all_to_all | solution.py:180
  50.6 1.9 %collective-permute-start.2 = (bf16[4,128,256]{2,1,0:T(8,128)(2,1)S(1)}, bf16[4,128,256]{2,1,0:T(8,128)(2,1)S(1)}, u32[]{:S(2)}, u32[]{:S(2)}) collective-permute-start(bf16[4,128,256]{2,1,0:T(8,128)(2,1)S(1)} %get-tuple-element.24), channel_id=1, source_target_pairs={{0,1},{1,0},{2,3},{3,2},{4,5},{5,4},{6,7},{7,6},{8,9},{9,8},{10,11... | collective-permute-start | bytes 786440 | tf_op jit(solution)/shard_map/ppermute | solution.py:167
  52.5 1.5 %collective-permute-done.2 = bf16[4,128,256]{2,1,0:T(8,128)(2,1)S(1)} collective-permute-done((bf16[4,128,256]{2,1,0:T(8,128)(2,1)S(1)}, bf16[4,128,256]{2,1,0:T(8,128)(2,1)S(1)}, u32[]{:S(2)}, u32[]{:S(2)}) %collective-permute-start.2) | collective-permute-done | bytes 262176 | tf_op jit(solution)/shard_map/ppermute | solution.py:167
  54.1 5.0 %collective-permute-start.3 = (f32[2,128,256]{2,1,0:T(8,128)S(1)}, f32[2,128,256]{2,1,0:T(8,128)S(1)}, u32[]{:S(2)}, u32[]{:S(2)}) collective-permute-start(f32[2,128,256]{2,1,0:T(8,128)S(1)} %slice.22), channel_id=1, source_target_pairs={{0,4},{2,6},{4,0},{6,2},{1,5},{3,7},{5,1},{7,3},{8,12},{10,14},{12... | collective-permute-start | bytes 786440 | tf_op jit(solution)/shard_map/ppermute | solution.py:167
  59.1 0.7 all-to-all-done
  59.9 0.7 broadcast_in_dim.24
  60.5 7.7 %all-to-all-start.1 = ((bf16[4,64,256]{2,1,0:T(8,128)(2,1)}), bf16[4,64,256]{2,1,0:T(8,128)(2,1)S(1)}, u32[]{:S(2)}, u32[]{:S(2)}) async-start(bf16[4,64,256]{2,1,0:T(8,128)(2,1)} %broadcast_in_dim.24), calls=%async_computation.1 | async-start | bytes 262144 | tf_op jit(solution)/shard_map/all_to_all | solution.py:172
  68.2 0.4 collective-permute-done.3
  68.6 8.7 %all-to-all-done.1 = bf16[4,64,256]{2,1,0:T(8,128)(2,1)S(1)} async-done(((bf16[4,64,256]{2,1,0:T(8,128)(2,1)}), bf16[4,64,256]{2,1,0:T(8,128)(2,1)S(1)}, u32[]{:S(2)}, u32[]{:S(2)}) %all-to-all-start.1) | async-done | bytes 131104 | tf_op jit(solution)/shard_map/all_to_all | solution.py:172
  77.3 0.8 broadcast_in_dim.25
  78.2 5.4 %all-to-all-start.2 = ((bf16[16,64,256]{2,1,0:T(8,128)(2,1)}), bf16[16,64,256]{2,1,0:T(8,128)(2,1)S(1)}, u32[]{:S(2)}, u32[]{:S(2)}) async-start(bf16[16,64,256]{2,1,0:T(8,128)(2,1)} %broadcast_in_dim.25), calls=%async_computation.2 | async-start | bytes 1048576 | tf_op jit(solution)/shard_map/all_to_all | solution.py:172
  83.6 3.9 %collective-permute-start.4 = (bf16[128,256]{1,0:T(8,128)(2,1)S(1)}, bf16[128,256]{1,0:T(8,128)(2,1)S(1)}, u32[]{:S(2)}, u32[]{:S(2)}) collective-permute-start(bf16[128,256]{1,0:T(8,128)(2,1)S(1)} %fusion.1), channel_id=1, source_target_pairs={{0,2},{2,0},{4,6},{6,4},{1,3},{3,1},{5,7},{7,5},{8,10},{10,8},{12,... | collective-permute-start | bytes 196616 | tf_op jit(solution)/shard_map/ppermute | solution.py:167
  87.5 5.2 %all-to-all-done.2 = bf16[16,64,256]{2,1,0:T(8,128)(2,1)S(1)} async-done(((bf16[16,64,256]{2,1,0:T(8,128)(2,1)}), bf16[16,64,256]{2,1,0:T(8,128)(2,1)S(1)}, u32[]{:S(2)}, u32[]{:S(2)}) %all-to-all-start.2) | async-done | bytes 524320 | tf_op jit(solution)/shard_map/all_to_all | solution.py:172
  92.7 1.1 %bitcast_convert_fusion = f32[1024,256]{1,0:T(8,128)} fusion(bf16[16,64,256]{2,1,0:T(8,128)(2,1)S(1)} %all-to-all-done.2), kind=kLoop, calls=%fused_computation | loop fusion | flops 262144 | bytes 1572864 | tf_op jit(solution)/shard_map/convert_element_type | solution.py:210
  93.8 0.7 fusion
  (24 shorter events, 0.3 us)
Async XLA Ops:
  0.6 0.7 copy-start.3
  0.6 1.5 %copy-start.2 = (bf16[128,256]{1,0:T(8,128)(2,1)S(1)}, bf16[128,256]{1,0:T(8,128)(2,1)}, u32[]{:S(2)}) copy-start(bf16[128,256]{1,0:T(8,128)(2,1)} %param.7) | copy-start | bytes 196612
  2.2 11.4 %collective-permute-start = (bf16[160,256]{1,0:T(8,128)(2,1)S(1)}, bf16[160,256]{1,0:T(8,128)(2,1)S(1)}, u32[]{:S(2)}, u32[]{:S(2)}) collective-permute-start(bf16[160,256]{1,0:T(8,128)(2,1)S(1)} %constant_dynamic-update-slice_fusion.block_ref.block_a), channel_id=1, source_target_pairs={{0,256},{256,0},{1,257},{257,1},{2,258},{258,2},{3,259},{259,3},{4... | collective-permute-start | bytes 245768 | tf_op jit(solution)/shard_map/ppermute | solution.py:167
  10.0 1.2 %copy-start = (f32[1024,256]{1,0:T(8,128)S(1)}, f32[1024,256]{1,0:T(8,128)}, u32[]{:S(2)}) copy-start(f32[1024,256]{1,0:T(8,128)} %table_ref.3) | copy-start | bytes 3145732
  13.1 23.6 %copy-start.1 = (f32[1024,256]{1,0:T(8,128)S(1)}, f32[1024,256]{1,0:T(8,128)}, u32[]{:S(2)}) copy-start(f32[1024,256]{1,0:T(8,128)} %table_ref.3) | copy-start | bytes 3145732
  34.8 3.9 %collective-permute-start.1 = (bf16[4,256,256]{2,1,0:T(8,128)(2,1)S(1)}, bf16[4,256,256]{2,1,0:T(8,128)(2,1)S(1)}, u32[]{:S(2)}, u32[]{:S(2)}) collective-permute-start(bf16[4,256,256]{2,1,0:T(8,128)(2,1)S(1)} %bitcast.16), channel_id=1, source_target_pairs={{0,1},{1,0},{2,3},{3,2},{4,5},{5,4},{6,7},{7,6},{8,9},{9,8},{10,11... | collective-permute-start | bytes 1572872 | tf_op jit(solution)/shard_map/ppermute | solution.py:167
  43.6 16.2 %all-to-all-start = ((bf16[16,64,256]{2,1,0:T(8,128)(2,1)}), bf16[16,64,256]{2,1,0:T(8,128)(2,1)S(1)}, u32[]{:S(2)}, u32[]{:S(2)}) async-start(bf16[16,64,256]{2,1,0:T(8,128)(2,1)} %get-tuple-element.25), calls=%async_computation | async-start | bytes 1048576 | tf_op jit(solution)/shard_map/all_to_all | solution.py:180
  50.6 3.4 %collective-permute-start.2 = (bf16[4,128,256]{2,1,0:T(8,128)(2,1)S(1)}, bf16[4,128,256]{2,1,0:T(8,128)(2,1)S(1)}, u32[]{:S(2)}, u32[]{:S(2)}) collective-permute-start(bf16[4,128,256]{2,1,0:T(8,128)(2,1)S(1)} %get-tuple-element.24), channel_id=1, source_target_pairs={{0,1},{1,0},{2,3},{3,2},{4,5},{5,4},{6,7},{7,6},{8,9},{9,8},{10,11... | collective-permute-start | bytes 786440 | tf_op jit(solution)/shard_map/ppermute | solution.py:167
  54.1 14.4 %collective-permute-start.3 = (f32[2,128,256]{2,1,0:T(8,128)S(1)}, f32[2,128,256]{2,1,0:T(8,128)S(1)}, u32[]{:S(2)}, u32[]{:S(2)}) collective-permute-start(f32[2,128,256]{2,1,0:T(8,128)S(1)} %slice.22), channel_id=1, source_target_pairs={{0,4},{2,6},{4,0},{6,2},{1,5},{3,7},{5,1},{7,3},{8,12},{10,14},{12... | collective-permute-start | bytes 786440 | tf_op jit(solution)/shard_map/ppermute | solution.py:167
  60.5 16.8 %all-to-all-start.1 = ((bf16[4,64,256]{2,1,0:T(8,128)(2,1)}), bf16[4,64,256]{2,1,0:T(8,128)(2,1)S(1)}, u32[]{:S(2)}, u32[]{:S(2)}) async-start(bf16[4,64,256]{2,1,0:T(8,128)(2,1)} %broadcast_in_dim.24), calls=%async_computation.1 | async-start | bytes 262144 | tf_op jit(solution)/shard_map/all_to_all | solution.py:172
  78.2 14.6 %all-to-all-start.2 = ((bf16[16,64,256]{2,1,0:T(8,128)(2,1)}), bf16[16,64,256]{2,1,0:T(8,128)(2,1)S(1)}, u32[]{:S(2)}, u32[]{:S(2)}) async-start(bf16[16,64,256]{2,1,0:T(8,128)(2,1)} %broadcast_in_dim.25), calls=%async_computation.2 | async-start | bytes 1048576 | tf_op jit(solution)/shard_map/all_to_all | solution.py:172
  83.6 10.2 %collective-permute-start.4 = (bf16[128,256]{1,0:T(8,128)(2,1)S(1)}, bf16[128,256]{1,0:T(8,128)(2,1)S(1)}, u32[]{:S(2)}, u32[]{:S(2)}) collective-permute-start(bf16[128,256]{1,0:T(8,128)(2,1)S(1)} %fusion.1), channel_id=1, source_target_pairs={{0,2},{2,0},{4,6},{6,4},{1,3},{3,1},{5,7},{7,5},{8,10},{10,8},{12,... | collective-permute-start | bytes 196616 | tf_op jit(solution)/shard_map/ppermute | solution.py:167
